TPU v7x, 512 devices: a whole 4x4x16 slice. The times are simulated.
512 devices in a mesh: head: 8 (over x_hi, y), seq: 64 (over z, x_lo, core).
Axes of the slice: x: 4 (x_hi: 2, x_lo: 2; x = x_hi * 2 + x_lo), y: 4, z: 16, core: 2. Of those that a mesh axis runs over, the one named last changes fastest.
Arguments:
- queries: bfloat16 [8, 16384, 128], P('head', 'seq'), may hold values from -80 to 80
- keys: bfloat16 [8, 24576, 128], P('head', 'seq'), may hold values from -24 to 24
- head_pick: int32 [8], P('head'), may hold values from 0 to 63
- block_offset: int32 [8], P('head'), may hold values from 0 to 64, as said below
- owner_map: int32 [192], replicated, may hold values from 0 to 191, each once
Outputs:
- block_mass: float32 [8, 192, 128], P('head', 'seq')
Inputs may be any that keep to these rules, and one draw needn't show every extreme that they name: Query row r of group g stands at prompt position 128 * block_offset[g] + r. `owner_map`: names each key block once.
All inputs are finite; a program needn't handle non-finite values.
Results may differ from a plain program's by a relative error of at most 0.0003.
Values may be sent and summed in bfloat16 or wider, within the bound.
A program may use at most 64 MiB of HBM per device.

v0:
```python
import jax
import jax.numpy as jnp
from jax import lax
from jax.sharding import PartitionSpec as P

QH = 64
KV = 8
BLK = 128


NEGATIVE = -1e30


def span_of(length, quantum):
    best = quantum
    limit = min(length, 2048)
    for width in range(quantum, limit + 1, quantum):
        if length % width == 0:
            best = width
    return best


def tile_scores(query_rows, key_rows, query_positions, key_positions):
    raw = lax.dot_general(
        query_rows, key_rows, (((1,), (1,)), ((), ())), preferred_element_type=jnp.float32
    )
    scaled = raw * query_rows.shape[1] ** (-0.5)
    allowed = key_positions[None, :] <= query_positions[:, None]
    return (jnp.where(allowed, scaled, NEGATIVE), allowed)


def fold_stats(row_top, row_sum, masked, allowed):
    new_top = jnp.maximum(row_top, jnp.max(masked, axis=1))
    weights = jnp.where(allowed, jnp.exp(masked - new_top[:, None]), 0.0)
    return (new_top, row_sum * jnp.exp(row_top - new_top) + jnp.sum(weights, axis=1), weights)


def add_blocks(block_sums, weights, first):
    sums = weights.reshape(weights.shape[0], -1, BLK).sum(axis=2)
    column = first // BLK
    current = lax.dynamic_slice_in_dim(block_sums, column, sums.shape[1], 1)
    return lax.dynamic_update_slice_in_dim(block_sums, current + sums, column, 1)


def body(queries, keys, head_pick, block_offset, owner_map):
    seq_count = lax.axis_size("seq")
    seq_rank = lax.axis_index("seq")
    own_rows = queries[0]
    query_count = own_rows.shape[0]
    key_count = keys.shape[1]
    key_blocks = key_count * seq_count // BLK
    every_head = lax.all_gather(keys, "head", axis=0, tiled=True)
    shared_index = head_pick[0] // (QH // KV)
    chosen = lax.dynamic_index_in_dim(every_head, shared_index, 0, keepdims=False)
    first_position = block_offset[0] * BLK
    query_positions = (
        first_position + seq_rank * query_count + jnp.arange(query_count, dtype=jnp.int32)
    )

    def visit_tiles(carry, piece, update):
        length = piece.shape[0]
        span = span_of(length, BLK)
        tiles = piece.reshape(length // span, span, piece.shape[1])

        def advance(state, entry):
            number, tile = entry
            first = number * span
            key_positions = first + jnp.arange(span, dtype=jnp.int32)
            masked, allowed = tile_scores(own_rows, tile, query_positions, key_positions)
            return (update(state, masked, allowed, first), None)

        result, unused = lax.scan(
            advance, carry, (jnp.arange(length // span, dtype=jnp.int32), tiles)
        )
        return result

    empty_top = jnp.full((query_count,), NEGATIVE, jnp.float32)
    empty_sum = jnp.zeros((query_count,), jnp.float32)
    empty_blocks = jnp.zeros((query_count, key_blocks), jnp.float32)

    def stats_update(state, masked, allowed, first):
        new_top, new_sum, unused = fold_stats(state[0], state[1], masked, allowed)
        return (new_top, new_sum)

    row_top, row_sum = visit_tiles(
        (empty_top, empty_sum), lax.all_gather(chosen, "seq", axis=0, tiled=True), stats_update
    )
    inverse = 1.0 / row_sum

    def mass_update(block_sums, masked, allowed, first):
        weights = jnp.where(allowed, jnp.exp(masked - row_top[:, None]), 0.0) * inverse[:, None]
        return add_blocks(block_sums, weights, first)

    row_mass = visit_tiles(
        empty_blocks, lax.all_gather(chosen, "seq", axis=0, tiled=True), mass_update
    )
    query_mass = row_mass.reshape(query_count // BLK, BLK, key_blocks).sum(axis=1)
    ordered = jnp.take(query_mass.T, owner_map, axis=0)
    delivered = lax.all_to_all(ordered, "seq", split_axis=0, concat_axis=1, tiled=True)
    return delivered[None]


def solution(mesh):
    return jax.shard_map(
        body,
        mesh=mesh,
        in_specs=(P("head", "seq", None), P("head", "seq", None), P("head"), P("head"), P()),
        out_specs=P("head", "seq", None),
        check_vma=False,
    )
```

profile of v0, /device:TPU:1, one launch (start us, length us, event | category | flops | bytes accessed | tf_op | source)
XLA Modules:
  0.0 290.5 jit_solution(1479477206281322869)
XLA Ops:
  7.2 32.3 %all_gather.7 = bf16[8,384,128]{2,1,0:T(8,128)(2,1)S(1)} all-gather(bf16[1,384,128]{2,1,0:T(8,128)(2,1)} %param.10), channel_id=1, replica_groups=mesh['head'=8,'seq'=64] {'head'}, dimensions={0}, use_global_device_ids=true | all-gather | bytes 884736 | tf_op jit(solution)/shard_map/all_gather | solution.py:52
  40.9 0.7 compare_and_fusion
  41.7 0.7 compare_select_fusion.1
  42.4 134.0 %all-gather.3.cloned.1.call-done = bf16[1,24576,128]{2,1,0:T(8,128)(2,1)} async-done(((bf16[1,384,128]{2,1,0:T(8,128)(2,1)}), bf16[1,24576,128]{2,1,0:T(8,128)(2,1)}) %all-gather.3.cloned.1.call-update) | async-done | bytes 6291472 | tf_op jit(solution)/shard_map/all_gather | solution.py:95
  176.5 41.5 %while.27 = (s32[]{:T(128)}, f32[256]{0:T(256)S(1)}, f32[256]{0:T(256)S(1)}, s32[12]{0:T(128)S(1)}, bf16[12,2048,128]{2,1,0:T(8,128)(2,1)}, /*index=5*/bf16[256,...) while((s32[]{:T(128)}, f32[256]{0:T(256)S(1)}, f32[256]{0:T(256)S(1)}, ...), condition=%wide.region_3.4_spmd.clone, body=%wide.region_0.3_spmd.clone.sunk | while | flops 138415616 | bytes 4825744 | solution.py:72
  177.7 1.7 fusion.34
  181.1 1.7 fusion.34
  184.6 1.7 fusion.34
  188.0 1.7 fusion.34
  191.5 1.7 fusion.34
  194.9 1.7 fusion.34
  198.4 1.7 fusion.34
  201.9 1.7 fusion.34
  205.3 1.7 fusion.34
  208.8 1.7 fusion.34
  212.2 1.7 fusion.34
  215.7 1.7 fusion.34
  218.0 40.7 %while.26 = (s32[]{:T(128)}, f32[256,192]{0,1:T(8,128)S(1)}, s32[12]{0:T(128)S(1)}, bf16[12,2048,128]{2,1,0:T(8,128)(2,1)}, bf16[256,128]{1,0:T(8,128)(2,1)}, /*...) while((s32[]{:T(128)}, f32[256,192]{0,1:T(8,128)S(1)}, ...), condition=%wide.region_6.7_spmd.clone, body=%wide.region_4.6_spmd.clone.sunk | while | flops 137890048 | bytes 709485 | solution.py:72
  219.2 1.9 bitcast_reduce_fusion.3
  222.6 1.9 bitcast_reduce_fusion.3
  226.0 1.9 bitcast_reduce_fusion.3
  229.4 1.9 bitcast_reduce_fusion.3
  232.8 1.9 bitcast_reduce_fusion.3
  236.2 1.9 bitcast_reduce_fusion.3
  239.6 1.9 bitcast_reduce_fusion.3
  243.0 1.9 bitcast_reduce_fusion.3
  246.4 1.9 bitcast_reduce_fusion.3
  249.8 1.9 bitcast_reduce_fusion.3
  253.2 1.9 bitcast_reduce_fusion.3
  256.6 1.9 bitcast_reduce_fusion.3
  259.0 0.7 gather_fusion
  260.0 23.0 %all_to_all.13 = f32[64,3,2]{1,2,0:T(2,128)S(1)} all-to-all(f32[64,3,2]{1,2,0:T(2,128)S(1)} %copy.13), channel_id=1, replica_groups=mesh['head'=8,'seq'=64] {'seq'}, dimensions={0} | all-to-all | bytes 3072 | tf_op jit(solution)/shard_map/all_to_all | solution.py:99
  (163 shorter events, 25.7 us)
Async XLA Ops:
  6.5 169.9 %all-gather.3.cloned.1.call-start = ((), (), s32[]{:S(2)}) async-start(), calls=%async_computation.1 | async-start | bytes 6389760 | tf_op jit(solution)/shard_map/all_gather | solution.py:95
Sparse Core Ops, SparseCore 0:
  40.3 136.0 all-gather.2
where the time goes:
time: 291 us; the launch traced here: 290 us
  waiting for transfers between devices  134 us (46%)
  blocking collectives  55.3 us (19%)
  matrix products  42.9 us (15%)
  local copies, waits for them, and re-layouts  19.7 us (7%)
  loops' own time  15.6 us (5%)
  between operations  14.8 us (5%)
  other arithmetic  8.08 us (3%)
    all_gather x1, waiting for transfers between devices, body(): lax.all_gather(chosen, 'seq', axis=0, tiled=True)  134 us
    dot_general x24, matrix products, tile_scores(): lax.dot_general(query_rows, key_rows, (((1,), (1,)), ((), ())), preferred...  42.9 us
    all_gather x1, blocking collectives, body(): every_head = lax.all_gather(keys, 'head', axis=0, tiled=True)  32.3 us
    all_to_all x1, blocking collectives, body(): lax.all_to_all(ordered, 'seq', split_axis=0, concat_axis=1, tiled=True)  23 us
    another operation x2, loops' own time, visit_tiles(): lax.scan(advance, carry, (jnp.arange(length // span, dtype=jnp.int32), ti...  15.6 us
    dynamic_slice x24, local copies, waits for them, and re-layouts, visit_tiles(): lax.scan(advance, carry, (jnp.arange(length // span, dtype=jnp.int32), ti...  14.2 us
    reduce_sum x12, other arithmetic, fold_stats(): jnp.sum(weights, axis=1)  5.99 us
  transfers between devices with their start and end apart: 1, of which 1 were waited for; matrix products, arithmetic and copies ran while one was open for 1% of the time, Pallas kernels for 0%

commit v1 on v0

v1 whole, which is shorter than its diff:
```python
import functools

import jax
import jax.numpy as jnp
from jax import lax
from jax.experimental import pallas as pl
from jax.experimental.pallas import tpu as pltpu
from jax.sharding import PartitionSpec as P

QH = 64
KV = 8
HD = 128
BLK = 128
NH = 8
NZ = 16
PLANE = 4
Q_DEV = 256
K_DEV = 384
PIECE = K_DEV // NH
KBD = K_DEV // BLK
PKB = PLANE * KBD
HALF = NZ // 2
NEGATIVE = -1e30
SCALE2 = 1.4426950408889634 * HD**-0.5
MESH = pl.DeviceIdType.MESH


def kernel(
    q_ref, k_ref, pick_ref, off_ref, own_ref, o_ref,
    qall, kp, stage1, recv1, stage2, table, probs, maxes, stats, stat_in, reply_out, reply_in,
    mass_out, mass_in, picked, lanes, plane_out, plane_in,
    ring_send, ring_recv, s1_send, s1_recv, s2_send, s2_recv, s3_send, s3_recv,
    st_send, st_recv, rp_send, rp_recv, ms_send, ms_recv, pe_send, pe_recv,
):
    head = lax.axis_index("head")
    seq = lax.axis_index("seq")
    z = seq // PLANE
    cls = seq % PLANE
    xl = cls // 2
    core = cls % 2

    def at_z(other):
        return {"head": head, "seq": lax.rem(other + NZ, NZ) * PLANE + cls}

    def remote(src, dst, send, recv, device):
        return pltpu.make_async_remote_copy(
            src_ref=src, dst_ref=dst, send_sem=send, recv_sem=recv,
            device_id=device, device_id_type=MESH,
        )

    barrier = pltpu.get_barrier_semaphore()
    peers = 0
    for step in range(1, NZ):
        pl.semaphore_signal(barrier, inc=1, device_id=at_z(z + step), device_id_type=MESH)
        peers += 1
    for gi in range(NH):
        for xo in range(2):
            if gi or xo:
                target = {"head": lax.rem(head + gi, NH), "seq": z * PLANE + lax.rem(xl + xo, 2) * 2 + core}
                pl.semaphore_signal(barrier, inc=1, device_id=target, device_id_type=MESH)
                peers += 1
    for xo in range(2):
        target = {"head": head, "seq": z * PLANE + lax.rem(xl + xo, 2) * 2 + (1 - core)}
        pl.semaphore_signal(barrier, inc=1, device_id=target, device_id_type=MESH)
        peers += 1

    qall[z] = q_ref[...]
    picks = jnp.full((16, HD), (pick_ref[0] // (QH // KV)).astype(jnp.float32), jnp.float32).astype(jnp.bfloat16)
    for m in range(NH):
        stage1[m, 0:PIECE, :] = k_ref[m * PIECE:(m + 1) * PIECE, :]
        stage1[m, PIECE:PIECE + 16, :] = picks
    recv1[head] = stage1[head]
    key_local = lax.broadcasted_iota(jnp.int32, (BLK, BLK), 0)
    query_local = lax.broadcasted_iota(jnp.int32, (BLK, BLK), 1)
    table[0] = jnp.full((BLK, BLK), NEGATIVE, jnp.float32)
    table[1] = jnp.where(key_local <= query_local, 0.0, NEGATIVE)
    table[2] = jnp.zeros((BLK, BLK), jnp.float32)
    probs[...] = jnp.zeros_like(probs)
    stats[...] = jnp.zeros_like(stats)

    pl.semaphore_wait(barrier, peers)

    def ring_copy(direction, d):
        sign = 1 if direction == 0 else -1
        slot = lax.rem(z - sign * (d - 1) + NZ, NZ)
        if d == HALF:
            rows = pl.ds(direction * BLK, BLK)
            ref = qall.at[slot, rows, :]
        else:
            ref = qall.at[slot]
        return remote(
            ref, ref, ring_send.at[direction, d - 1], ring_recv.at[direction, d - 1], at_z(z + sign)
        )

    def ring_arrival(direction, d):
        sign = 1 if direction == 0 else -1
        slot = lax.rem(z - sign * d + NZ, NZ)
        if d == HALF:
            ref = qall.at[slot, pl.ds(direction * BLK, BLK), :]
        else:
            ref = qall.at[slot]
        return remote(
            ref, ref, ring_send.at[direction, d - 1], ring_recv.at[direction, d - 1], at_z(z + sign)
        )

    def ring_step(d):
        for direction in range(2):
            ring_arrival(direction, d).wait_recv()
            if d < HALF:
                ring_copy(direction, d + 1).start()

    def s1_copy(i):
        other = lax.rem(head + i, NH)
        return remote(
            stage1.at[other], recv1.at[head], s1_send.at[i], s1_recv.at[i], {"head": other, "seq": seq}
        )

    def s1_arrival(i):
        other = lax.rem(head - i + NH, NH)
        return remote(
            stage1.at[other], recv1.at[other], s1_send.at[i], s1_recv.at[i], {"head": other, "seq": seq}
        )

    def s2_copy(gi, xo):
        other = lax.rem(head + gi, NH)
        target = {"head": other, "seq": z * PLANE + lax.rem(xl + xo, 2) * 2 + core}
        return remote(
            stage2.at[other], kp.at[pl.ds(cls * K_DEV + head * PIECE, PIECE), :],
            s2_send.at[gi, xo], s2_recv.at[gi, xo], target,
        )

    def s2_arrival(gi, xo):
        other = lax.rem(head - gi + NH, NH)
        ox = lax.rem(xl + xo, 2)
        source = {"head": other, "seq": z * PLANE + ox * 2 + core}
        return remote(
            stage2.at[other], kp.at[pl.ds((ox * 2 + core) * K_DEV + other * PIECE, PIECE), :],
            s2_send.at[gi, xo], s2_recv.at[gi, xo], source,
        )

    partner = {"head": head, "seq": z * PLANE + xl * 2 + (1 - core)}

    def s3_copy(xo, c):
        ref = kp.at[pl.ds((2 * xo + c) * K_DEV, K_DEV), :]
        return remote(ref, ref, s3_send.at[xo], s3_recv.at[xo], partner)

    for direction in range(2):
        ring_copy(direction, 1).start()
    for i in range(1, NH):
        s1_copy(i).start()
    ring_step(1)
    for i in range(1, NH):
        s1_arrival(i).wait_recv()
    pieces = [recv1[m, 0:PIECE, :].astype(jnp.float32) for m in range(NH)]
    for g in range(NH):
        wanted = recv1[g, PIECE:PIECE + 16, :].astype(jnp.float32)[0:8]
        wanted = jnp.concatenate([wanted] * (PIECE // 8), axis=0)
        chosen = pieces[0]
        for m in range(1, NH):
            chosen = jnp.where(wanted == float(m), pieces[m], chosen)
        stage2[g] = chosen.astype(jnp.bfloat16)
    kp[pl.ds(cls * K_DEV + head * PIECE, PIECE), :] = stage2[head]
    s2_pairs = [(gi, xo) for gi in range(NH) for xo in range(2) if gi or xo]
    for gi, xo in s2_pairs:
        s2_copy(gi, xo).start()
    ring_step(2)
    for gi, xo in s2_pairs:
        s2_arrival(gi, xo).wait_recv()
    for xo in range(2):
        s3_copy(xo, core).start()
    ring_step(3)
    for xo in range(2):
        s3_copy(xo, 1 - core).wait_recv()

    offset = off_ref[0]

    def compute(item, unused):
        d = (item + 1) // 2
        down = 1 - lax.rem(item, 2)
        signed = jnp.where(down == 1, d, -d)
        slot = lax.rem(z + signed + NZ, NZ)
        q = qall[slot]
        blocks = [[], []]
        for kb in range(PKB):
            s = lax.dot_general(
                kp[kb * BLK:(kb + 1) * BLK, :], q, (((1,), (1,)), ((), ())),
                preferred_element_type=jnp.float32,
            )
            for j in range(2):
                ahead = slot * 8 + cls * 2 + j + offset - (z * PKB + kb)
                which = jnp.clip(ahead + 1, 0, 2)
                sj = s[:, j * BLK:(j + 1) * BLK] + table[which]
                top = jnp.max(sj, axis=0, keepdims=True)
                total = jnp.sum(jnp.exp2((sj - top) * SCALE2), axis=0, keepdims=True)
                row = 4 * (kb // KBD) + kb % KBD
                maxes[j, row:row + 1, :] = top
                probs[slot, j, row:row + 1, :] = total
        for j in range(2):
            tops = maxes[j]
            used = lax.rem(lax.broadcasted_iota(jnp.int32, (16, BLK), 0), 4) < KBD
            tops = jnp.where(used, tops, NEGATIVE)
            top = jnp.max(tops, axis=0, keepdims=True)
            scaled = jnp.where(used, probs[slot, j] * jnp.exp2((tops - top) * SCALE2), 0.0)
            probs[slot, j] = scaled
            stats[slot, 2 * j:2 * j + 1, :] = top
            stats[slot, 2 * j + 1:2 * j + 2, :] = jnp.sum(scaled, axis=0, keepdims=True)
        return unused

    def st_copy(r):
        slot = lax.rem(z + HALF + r, NZ)
        return remote(stats.at[slot], stat_in.at[z], st_send.at[r], st_recv.at[r], at_z(z + r))

    def st_arrival(r):
        source = lax.rem(z - r + NZ, NZ)
        return remote(stats.at[source], stat_in.at[source], st_send.at[r], st_recv.at[r], at_z(z + r))

    def send_stats(lo, hi):
        for item in range(lo, hi):
            d = (item + 1) // 2
            r = HALF - d if item % 2 == 1 or item == 0 else HALF + d
            st_copy(r).start()

    def run(lo, hi):
        lax.fori_loop(lo, hi, compute, 0)
        send_stats(lo, min(hi, 2 * HALF - 1))

    run(0, 3)
    ring_step(4)
    run(3, 7)
    ring_step(5)
    run(7, 10)
    ring_step(6)
    run(10, 13)
    ring_step(7)
    run(13, 15)
    ring_step(8)
    lax.fori_loop(15, 16, compute, 0)

    far = lax.rem(z + HALF, NZ)
    stat_in[z] = stats[far]
    for r in range(1, NZ):
        st_arrival(r).wait_recv()
    out_rows = []
    for j in range(2):
        tops = stat_in[:, 2 * j, :]
        top = jnp.max(tops, axis=0, keepdims=True)
        total = jnp.sum(stat_in[:, 2 * j + 1, :] * jnp.exp2((tops - top) * SCALE2), axis=0, keepdims=True)
        reply_out[2 * j:2 * j + 1, :] = top
        reply_out[2 * j + 1:2 * j + 2, :] = 1.0 / total
    reply_out[4:8, :] = jnp.zeros((4, BLK), jnp.float32)
    reply_in[far] = reply_out[...]

    def rp_copy(r):
        return remote(reply_out, reply_in.at[far], rp_send.at[r], rp_recv.at[r], at_z(z + r))

    def rp_arrival(r):
        slot = lax.rem(z - r + HALF + NZ, NZ)
        return remote(reply_out, reply_in.at[slot], rp_send.at[r], rp_recv.at[r], at_z(z + r))

    for r in range(1, NZ):
        rp_copy(r).start()

    lane = lax.broadcasted_iota(jnp.int32, (16, BLK), 1)
    mass = jnp.zeros((16, BLK), jnp.float32)
    order = [0]
    for d in range(1, HALF):
        order += [d, NZ - d]
    order.append(HALF)
    for r in order:
        if r:
            rp_arrival(r).wait_recv()
        slot = lax.rem(z - r + HALF + NZ, NZ)
        for j in range(2):
            top = reply_in[slot, 2 * j:2 * j + 1, :]
            weight = jnp.exp2((stats[slot, 2 * j:2 * j + 1, :] - top) * SCALE2) * reply_in[slot, 2 * j + 1:2 * j + 2, :]
            column = jnp.sum(probs[slot, j] * weight, axis=1, keepdims=True)
            mass = jnp.where(lane == slot * 2 + j, column, mass)
    packed = mass[0:4]
    for part in range(1, 4):
        packed = packed + pltpu.roll(mass[4 * part:4 * part + 4], 32 * part, 1)
    mass_out[...] = packed
    mass_in[z] = packed

    def ms_copy(r):
        return remote(mass_out, mass_in.at[z], ms_send.at[r], ms_recv.at[r], at_z(z + r))

    def ms_arrival(r):
        source = lax.rem(z - r + NZ, NZ)
        return remote(mass_out, mass_in.at[source], ms_send.at[r], ms_recv.at[r], at_z(z + r))

    for r in range(1, NZ):
        ms_copy(r).start()
    for c in range(PLANE):
        for t in range(KBD):
            block = own_ref[z * PKB + c * KBD + t]
            lanes[4 * c + t:4 * c + t + 1, :] = jnp.full((1, BLK), 32 * (lax.rem(block, PKB) // KBD), jnp.int32)
        lanes[4 * c + 3:4 * c + 4, :] = jnp.zeros((1, BLK), jnp.int32)
        picked[4 * c + 3:4 * c + 4, :] = jnp.zeros((1, BLK), jnp.float32)
    for r in range(1, NZ):
        ms_arrival(r).wait_recv()
    for c in range(PLANE):
        for t in range(KBD):
            block = own_ref[z * PKB + c * KBD + t]
            picked[4 * c + t:4 * c + t + 1, :] = mass_in[block // PKB, pl.ds(lax.rem(block, KBD), 1), :]
    where_from = lanes[...] + lane // 8 * 2 + lane % 2
    spread = jnp.take_along_axis(picked[...], where_from, axis=1)
    spread = jnp.where(lane // 2 % 4 == cls, spread, 0.0)
    for c in range(PLANE):
        plane_out[c] = spread[4 * c:4 * c + 4]
    plane_in[cls] = plane_out[cls]

    def pe_copy(i):
        other = lax.rem(cls + i, PLANE)
        return remote(
            plane_out.at[other], plane_in.at[cls], pe_send.at[i], pe_recv.at[i],
            {"head": head, "seq": z * PLANE + other},
        )

    def pe_arrival(i):
        other = lax.rem(cls - i + PLANE, PLANE)
        return remote(
            plane_out.at[other], plane_in.at[other], pe_send.at[i], pe_recv.at[i],
            {"head": head, "seq": z * PLANE + other},
        )

    for i in range(1, PLANE):
        pe_copy(i).start()
    for i in range(1, PLANE):
        pe_arrival(i).wait_recv()
    final = plane_in[0] + plane_in[1] + plane_in[2] + plane_in[3]
    o_ref[0] = final[0:KBD]

    for direction in range(2):
        for d in range(1, HALF + 1):
            ring_copy(direction, d).wait_send()
    for i in range(1, NH):
        s1_copy(i).wait_send()
    for gi, xo in s2_pairs:
        s2_copy(gi, xo).wait_send()
    for xo in range(2):
        s3_copy(xo, core).wait_send()
    for r in range(1, NZ):
        st_copy(r).wait_send()
        rp_copy(r).wait_send()
        ms_copy(r).wait_send()
    for i in range(1, PLANE):
        pe_copy(i).wait_send()


def body(queries, keys, head_pick, block_offset, owner_map):
    vmem = pl.BlockSpec(memory_space=pltpu.VMEM)
    smem = pl.BlockSpec(memory_space=pltpu.SMEM)
    f32, bf16 = jnp.float32, jnp.bfloat16
    dma = pltpu.SemaphoreType.DMA
    return pl.pallas_call(
        kernel,
        out_shape=jax.ShapeDtypeStruct((1, KBD, BLK), f32),
        in_specs=[vmem, vmem, smem, smem, smem],
        out_specs=vmem,
        scratch_shapes=[
            pltpu.VMEM((NZ, Q_DEV, HD), bf16),
            pltpu.VMEM((PLANE * K_DEV, HD), bf16),
            pltpu.VMEM((NH, PIECE + 16, HD), bf16),
            pltpu.VMEM((NH, PIECE + 16, HD), bf16),
            pltpu.VMEM((NH, PIECE, HD), bf16),
            pltpu.VMEM((3, BLK, BLK), f32),
            pltpu.VMEM((NZ, 2, 16, BLK), f32),
            pltpu.VMEM((2, 16, BLK), f32),
            pltpu.VMEM((NZ, 8, BLK), f32),
            pltpu.VMEM((NZ, 8, BLK), f32),
            pltpu.VMEM((8, BLK), f32),
            pltpu.VMEM((NZ, 8, BLK), f32),
            pltpu.VMEM((4, BLK), f32),
            pltpu.VMEM((NZ, 4, BLK), f32),
            pltpu.VMEM((16, BLK), f32),
            pltpu.VMEM((16, BLK), jnp.int32),
            pltpu.VMEM((PLANE, 4, BLK), f32),
            pltpu.VMEM((PLANE, 4, BLK), f32),
            dma((2, HALF)), dma((2, HALF)),
            dma((NH,)), dma((NH,)),
            dma((NH, 2)), dma((NH, 2)),
            dma((2,)), dma((2,)),
            dma((NZ,)), dma((NZ,)),
            dma((NZ,)), dma((NZ,)),
            dma((NZ,)), dma((NZ,)),
            dma((PLANE,)), dma((PLANE,)),
        ],
        compiler_params=pltpu.CompilerParams(
            collective_id=0, has_side_effects=True, vmem_limit_bytes=32 * 1024 * 1024
        ),
        cost_estimate=pl.CostEstimate(flops=1610612736, bytes_accessed=165000, transcendentals=6291456),
    )(queries[0], keys[0], head_pick, block_offset, owner_map)


def solution(mesh):
    return jax.shard_map(
        body,
        mesh=mesh,
        in_specs=(P("head", "seq", None), P("head", "seq", None), P("head"), P("head"), P()),
        out_specs=P("head", "seq", None),
        check_vma=False,
    )
```

time: 291 us -> 71.1 us (0.24)
  waiting for transfers between devices: 134 us -> 0 us
  Pallas kernels: 0 us -> 66.6 us
  blocking collectives: 55.3 us -> 0 us
  matrix products: 42.9 us -> 0 us
  local copies, waits for them, and re-layouts: 19.7 us -> 2.97 us
  loops' own time: 15.6 us -> 0 us
  between operations: 14.8 us -> 1.32 us
  other arithmetic: 8.08 us -> 0 us
    all_gather x1 -> x0, waiting for transfers between devices: 134 us -> none  [body(): lax.all_gather(chosen, 'seq', axis=0, tiled=True)]
    pallas_call x0 -> x1, Pallas kernels: none -> 66.6 us  [body(): pl.pallas_call(kernel, out_shape=jax.ShapeDtypeStruct((1, KBD, BLK), f32)...]
    dot_general x24 -> x0, matrix products: 42.9 us -> none  [tile_scores(): lax.dot_general(query_rows, key_rows, (((1,), (1,)), ((), ())), preferred...]
    all_gather x1 -> x0, blocking collectives: 32.3 us -> none  [body(): every_head = lax.all_gather(keys, 'head', axis=0, tiled=True)]
    all_to_all x1 -> x0, blocking collectives: 23 us -> none  [body(): lax.all_to_all(ordered, 'seq', split_axis=0, concat_axis=1, tiled=True)]
    another operation x2 -> x0, loops' own time: 15.6 us -> none  [visit_tiles(): lax.scan(advance, carry, (jnp.arange(length // span, dtype=jnp.int32), ti...]
    dynamic_slice x25 -> x0, local copies, waits for them, and re-layouts: 14.8 us -> none  [the longest x24 14.2 us: visit_tiles(): lax.scan(advance, carry, (jnp.arange(length // span, dtype=jnp.int32), ti...]
    reduce_sum x13 -> x0, other arithmetic: 6.03 us -> none  [the longest x12 5.99 us: fold_stats(): jnp.sum(weights, axis=1)]
  transfers between devices with their start and end apart: 1 -> 0, of which waited for: 1 -> 0; matrix products, arithmetic and copies ran while one was open for 1% -> 0% of each run, Pallas kernels for 0% -> 0%
where the time goes in v1:
time: 71.1 us; the launch traced here: 70.8 us
  Pallas kernels  66.6 us (94%)
  local copies, waits for them, and re-layouts  2.97 us (4%)
  between operations  1.32 us (2%)
    pallas_call x1, Pallas kernels, body(): pl.pallas_call(kernel, out_shape=jax.ShapeDtypeStruct((1, KBD, BLK), f32)...  66.6 us
    unnamed x6, local copies, waits for them, and re-layouts  2.4 us

profile of v1, /device:TPU:1, one launch (start us, length us, event | category | flops | bytes accessed | tf_op | source)
XLA Modules:
  0.0 70.8 jit_solution(17693258258354316607)
XLA Ops:
  1.3 0.0 copy-start.2
  1.3 0.7 copy-done.2
  2.0 0.0 copy-start
  2.0 0.9 %copy-done = bf16[1,384,128]{2,1,0:T(8,128)(2,1)S(1)} copy-done((bf16[1,384,128]{2,1,0:T(8,128)(2,1)S(1)}, bf16[1,384,128]{2,1,0:T(8,128)(2,1)}, u32[]{:S(2)}) %copy-start) | copy-done | bytes 98328
  2.9 0.0 copy-start.1
  2.9 0.8 %copy-done.1 = bf16[1,256,128]{2,1,0:T(8,128)(2,1)S(1)} copy-done((bf16[1,256,128]{2,1,0:T(8,128)(2,1)S(1)}, bf16[1,256,128]{2,1,0:T(8,128)(2,1)}, u32[]{:S(2)}) %copy-start.1) | copy-done | bytes 65560
  3.7 66.6 %shard_map.55 = f32[1,3,128]{2,1,0:T(4,128)S(1)} custom-call(bf16[256,128]{1,0:T(8,128)(2,1)S(1)} %bitcast.3, bf16[384,128]{1,0:T(8,128)(2,1)S(1)} %bitcast.2, s32[1]{0:T(128)S(6)} %copy.7.pick_ref, s32[1]{0:T(128)S(6)} %copy.8.off_ref, s32[192]{0:T(256)S(1)} %copy-done.2), custom_call_target="tpu_custom_call" | custom-call | flops 1610612736 | bytes 165000 | tf_op jit(solution)/shard_map/pallas_call | solution.py:355
  70.3 0.6 copy.6
Async XLA Ops:
  1.3 0.7 copy-start.2
  2.0 0.9 %copy-start = (bf16[1,384,128]{2,1,0:T(8,128)(2,1)S(1)}, bf16[1,384,128]{2,1,0:T(8,128)(2,1)}, u32[]{:S(2)}) copy-start(bf16[1,384,128]{2,1,0:T(8,128)(2,1)} %param.6) | copy-start | bytes 294916
  2.9 0.8 %copy-start.1 = (bf16[1,256,128]{2,1,0:T(8,128)(2,1)S(1)}, bf16[1,256,128]{2,1,0:T(8,128)(2,1)}, u32[]{:S(2)}) copy-start(bf16[1,256,128]{2,1,0:T(8,128)(2,1)} %param.5) | copy-start | bytes 196612

commit v2 on v0

v2 whole, which is shorter than its diff:
```python
import jax
import jax.numpy as jnp
from jax import lax
from jax.experimental import pallas as pl
from jax.experimental.pallas import tpu as pltpu
from jax.sharding import PartitionSpec as P

QH = 64
KV = 8
HD = 128
BLK = 128
NH = 8
NZ = 16
PLANE = 4
Q_DEV = 256
K_DEV = 384
PIECE = K_DEV // NH
KBD = K_DEV // BLK
PKB = PLANE * KBD
ROWS = 2 * PKB
HALF = NZ // 2
CHUNKS = 4
CHUNK = Q_DEV // CHUNKS
FIRST = 5
NEGATIVE = -1e30
SCALE2 = 1.4426950408889634 * HD**-0.5
MESH = pl.DeviceIdType.MESH


def kernel(
    q_ref, k_ref, pick_ref, off_ref, own_ref, o_ref,
    qall, kp, pick_out, picks, recv1, stage2, table, probs, tops, maxes, prob_in, top_in, weighted,
    mass_out, mass_in, plane_out, plane_in,
    local_sem, greet, ring_send, ring_recv, pk_send, pk_recv, s1_send, s1_recv, s2_send, s2_recv, s3_send, s3_recv,
    pr_send, pr_recv, tp_send, tp_recv, ms_send, ms_recv, pe_send, pe_recv,
):
    head = lax.axis_index("head")
    seq = lax.axis_index("seq")
    z = seq // PLANE
    cls = seq % PLANE
    xl = cls // 2
    core = cls % 2

    def wrap(other):
        return lax.rem(other + NZ, NZ)

    def at_z(other):
        return {"head": head, "seq": wrap(other) * PLANE + cls}

    def at_head(i):
        return {"head": lax.rem(head + i + NH, NH), "seq": seq}

    def at_pair(gi, xo):
        return {"head": lax.rem(head + gi + NH, NH), "seq": z * PLANE + lax.rem(xl + xo, 2) * 2 + core}

    def at_plane(c):
        return {"head": head, "seq": z * PLANE + lax.rem(c + PLANE, PLANE)}

    def remote(src, dst, send, recv, device):
        return pltpu.make_async_remote_copy(
            src_ref=src, dst_ref=dst, send_sem=send, recv_sem=recv,
            device_id=device, device_id_type=MESH,
        )

    def signal(sem, device):
        pl.semaphore_signal(sem, inc=1, device_id=device, device_id_type=MESH)

    barrier = pltpu.get_barrier_semaphore()
    s2_pairs = [(gi, xo) for gi in range(NH) for xo in range(2) if gi or xo]
    near = [at_z(z + 1), at_z(z - 1)]
    near += [at_pair(gi, xo) for gi, xo in s2_pairs]
    near += [{"head": head, "seq": z * PLANE + lax.rem(xl + xo, 2) * 2 + (1 - core)} for xo in range(2)]
    for device in near:
        signal(barrier, device)

    own_q = pltpu.make_async_copy(q_ref, qall.at[z], local_sem.at[0])
    own_k = pltpu.make_async_copy(k_ref.at[pl.ds(head * PIECE, PIECE), :], recv1.at[head], local_sem.at[1])
    own_q.start()
    own_k.start()
    picked = (pick_ref[0] // (QH // KV)).astype(jnp.float32)
    pick_out[...] = jnp.full((16, HD), picked, jnp.float32).astype(jnp.bfloat16)
    picks[head] = pick_out[...]

    pl.semaphore_wait(barrier, len(near))

    def ring_copy(direction, d, c, src=None):
        sign = 1 - 2 * direction
        ref = qall.at[wrap(z - sign * (d - 1)), pl.ds(c * CHUNK, CHUNK), :]
        return remote(
            ref if src is None else src, ref,
            ring_send.at[direction, d - 1, c], ring_recv.at[direction, d - 1, c], at_z(z + sign),
        )

    def ring_arrival(direction, d, c):
        sign = 1 - 2 * direction
        ref = qall.at[wrap(z - sign * d), pl.ds(c * CHUNK, CHUNK), :]
        return remote(
            ref, ref, ring_send.at[direction, d - 1, c], ring_recv.at[direction, d - 1, c], at_z(z + sign)
        )

    def first_ring_copy(direction, c):
        return ring_copy(direction, 1, c, q_ref.at[pl.ds(c * CHUNK, CHUNK), :])

    def serve(d, c):
        for direction in range(2):
            ring_arrival(direction, d, c).wait_recv()
            if isinstance(d, int):
                ring_copy(direction, d + 1, c).start()
            else:
                mine = c < CHUNKS // 2 if direction == 0 else c >= CHUNKS // 2

                @pl.when(jnp.logical_or(d < HALF - 1, mine))
                def _():
                    ring_copy(direction, d + 1, c).start()

    def ring_step(d):
        for c in range(CHUNKS):
            serve(d, c)

    def s1_copy(i):
        other = lax.rem(head + i, NH)
        return remote(
            k_ref.at[pl.ds(other * PIECE, PIECE), :], recv1.at[head], s1_send.at[i], s1_recv.at[i], at_head(i)
        )

    def s1_arrival(i):
        other = lax.rem(head - i + NH, NH)
        return remote(
            k_ref.at[pl.ds(other * PIECE, PIECE), :], recv1.at[other], s1_send.at[i], s1_recv.at[i], at_head(-i)
        )

    def pk_copy(i):
        return remote(pick_out, picks.at[head], pk_send.at[i], pk_recv.at[i], at_head(i))

    def pk_arrival(i):
        other = lax.rem(head - i + NH, NH)
        return remote(pick_out, picks.at[other], pk_send.at[i], pk_recv.at[i], at_head(-i))

    def s2_copy(gi, xo):
        other = lax.rem(head + gi, NH)
        return remote(
            stage2.at[other], kp.at[pl.ds(cls * K_DEV + head * PIECE, PIECE), :],
            s2_send.at[gi, xo], s2_recv.at[gi, xo], at_pair(gi, xo),
        )

    def s2_arrival(gi, xo):
        other = lax.rem(head - gi + NH, NH)
        start = (lax.rem(xl + xo, 2) * 2 + core) * K_DEV + other * PIECE
        return remote(
            stage2.at[other], kp.at[pl.ds(start, PIECE), :],
            s2_send.at[gi, xo], s2_recv.at[gi, xo], at_pair(-gi, xo),
        )

    def s3_copy(xo, c):
        ref = kp.at[pl.ds((2 * xo + c) * K_DEV, K_DEV), :]
        return remote(
            ref, ref, s3_send.at[xo], s3_recv.at[xo], {"head": head, "seq": z * PLANE + xl * 2 + (1 - core)}
        )

    for i in range(1, NH):
        pk_copy(i).start()
    for c in range(CHUNKS):
        for direction in range(2):
            first_ring_copy(direction, c).start()
    for i in range(1, NH):
        s1_copy(i).start()
    for side in range(2):
        signal(greet.at[0, side], at_z(z + 1 - 2 * side))

    key_local = lax.broadcasted_iota(jnp.int32, (BLK, BLK), 0)
    query_local = lax.broadcasted_iota(jnp.int32, (BLK, BLK), 1)
    table[0] = jnp.full((BLK, BLK), NEGATIVE, jnp.float32)
    table[1] = jnp.where(key_local <= query_local, 0.0, NEGATIVE)
    table[2] = jnp.zeros((BLK, BLK), jnp.float32)

    ring_step(1)
    for side in range(2):
        pl.semaphore_wait(greet.at[0, side], 1)
    for side in range(2):
        signal(greet.at[1, side], at_z(z + 2 - 4 * side))
    own_k.wait()
    for i in range(1, NH):
        pk_arrival(i).wait_recv()
        s1_arrival(i).wait_recv()
    pieces = [recv1[m].astype(jnp.float32) for m in range(NH)]
    for g in range(NH):
        wanted = picks[g].astype(jnp.float32)[0:8]
        wanted = jnp.concatenate([wanted] * (PIECE // 8), axis=0)
        chosen = pieces[0]
        for m in range(1, NH):
            chosen = jnp.where(wanted == float(m), pieces[m], chosen)
        stage2[g] = chosen.astype(jnp.bfloat16)
    for gi, xo in s2_pairs:
        s2_copy(gi, xo).start()
    kp[pl.ds(cls * K_DEV + head * PIECE, PIECE), :] = stage2[head]
    ring_step(2)
    for side in range(2):
        pl.semaphore_wait(greet.at[1, side], 1)
    for side in range(2):
        signal(greet.at[2, side], at_z(z + 4 - 8 * side))
    ring_step(3)
    for gi, xo in s2_pairs:
        s2_arrival(gi, xo).wait_recv()
    for xo in range(2):
        s3_copy(xo, core).start()
    ring_step(4)
    for side in range(2):
        pl.semaphore_wait(greet.at[2, side], 1)
    for xo in range(2):
        s3_copy(xo, 1 - core).wait_recv()
    own_q.wait()

    offset = off_ref[0]
    far = wrap(z + HALF)

    def pr_copy(r):
        return remote(probs.at[wrap(z + HALF + r)], prob_in.at[z], pr_send.at[r], pr_recv.at[r], at_z(z + r))

    def tp_copy(r):
        return remote(tops.at[wrap(z + HALF + r)], top_in.at[z], tp_send.at[r], tp_recv.at[r], at_z(z + r))

    def pr_arrival(r):
        source = wrap(z - r)
        return remote(probs.at[source], prob_in.at[source], pr_send.at[r], pr_recv.at[r], at_z(z - r))

    def tp_arrival(r):
        source = wrap(z - r)
        return remote(tops.at[source], top_in.at[source], tp_send.at[r], tp_recv.at[r], at_z(z - r))

    def compute(item, unused):
        later = HALF * 2 - CHUNKS

        @pl.when(item < later)
        def _():
            serve(FIRST + item // CHUNKS, lax.rem(item, CHUNKS))

        @pl.when(item == 2 * HALF - 1)
        def _():
            for c in range(CHUNKS):
                ring_arrival(2 * c // CHUNKS, HALF, c).wait_recv()

        d = (item + 1) // 2
        signed = jnp.where(lax.rem(item, 2) == 1, -d, d)
        slot = wrap(z + signed)
        q = qall[slot]
        for kb in range(PKB):
            s = lax.dot_general(
                kp[kb * BLK:(kb + 1) * BLK, :], q, (((1,), (1,)), ((), ())),
                preferred_element_type=jnp.float32,
            )
            for j in range(2):
                ahead = slot * 8 + cls * 2 + j + offset - (z * PKB + kb)
                sj = s[:, j * BLK:(j + 1) * BLK] + table[jnp.clip(ahead + 1, 0, 2)]
                top = jnp.max(sj, axis=0, keepdims=True)
                row = j * PKB + kb
                maxes[row:row + 1, :] = top
                probs[slot, row:row + 1, :] = jnp.sum(jnp.exp2((sj - top) * SCALE2), axis=0, keepdims=True)
        first = lax.broadcasted_iota(jnp.int32, (ROWS, BLK), 0) < PKB
        every = maxes[...]
        top0 = jnp.max(jnp.where(first, every, NEGATIVE), axis=0, keepdims=True)
        top1 = jnp.max(jnp.where(first, NEGATIVE, every), axis=0, keepdims=True)
        tops[slot, 0:1, :] = top0
        tops[slot, 1:2, :] = top1
        probs[slot] = probs[slot] * jnp.exp2((every - jnp.where(first, top0, top1)) * SCALE2)
        r = HALF + signed

        @pl.when(item < 2 * HALF - 1)
        def _():
            pr_copy(r).start()
            tp_copy(r).start()

        return unused

    lax.fori_loop(0, 2 * HALF, compute, 0)

    prob_in[z] = probs[far]
    top_in[z] = tops[far]
    for direction in range(2):
        for d in range(1, HALF):
            for c in range(CHUNKS):
                (first_ring_copy(direction, c) if d == 1 else ring_copy(direction, d, c)).wait_send()
    for i in range(1, NH):
        pk_copy(i).wait_send()
        s1_copy(i).wait_send()
    for gi, xo in s2_pairs:
        s2_copy(gi, xo).wait_send()
    for xo in range(2):
        s3_copy(xo, core).wait_send()
    for r in range(1, NZ):
        tp_arrival(r).wait_recv()
        pr_arrival(r).wait_recv()
    each = top_in[...]
    top = jnp.max(each, axis=0, keepdims=True)
    factor = jnp.exp2((each - top) * SCALE2)
    first = lax.broadcasted_iota(jnp.int32, (ROWS, BLK), 0) < PKB
    total = jnp.zeros((ROWS, BLK), jnp.float32)
    for source in range(NZ):
        part = prob_in[source] * jnp.where(first, factor[source, 0:1], factor[source, 1:2])
        total = total + part
        weighted[source * ROWS:(source + 1) * ROWS, :] = part
    sum0 = jnp.sum(jnp.where(first, total, 0.0), axis=0, keepdims=True)
    sum1 = jnp.sum(jnp.where(first, 0.0, total), axis=0, keepdims=True)
    inverse = 1.0 / jnp.where(lax.broadcasted_iota(jnp.int32, (8, BLK), 0) == 0, sum0, sum1)
    mass = lax.dot_general(
        inverse, weighted[...], (((1,), (1,)), ((), ())),
        precision=lax.Precision.HIGHEST, preferred_element_type=jnp.float32,
    )
    column = lax.broadcasted_iota(jnp.int32, (1, NZ * ROWS), 1)
    mass_out[...] = jnp.where(lax.rem(column, ROWS) < PKB, mass[0:1], mass[1:2])
    mass_in[far] = mass_out[...]

    def ms_copy(r):
        return remote(mass_out, mass_in.at[far], ms_send.at[r], ms_recv.at[r], at_z(z + r))

    def ms_arrival(r):
        source = wrap(z - r + HALF)
        return remote(mass_out, mass_in.at[source], ms_send.at[r], ms_recv.at[r], at_z(z - r))

    for d in range(HALF):
        ms_copy(HALF - d).start()
        if d:
            ms_copy(HALF + d).start()
    wide = lax.broadcasted_iota(jnp.int32, (8, NZ * ROWS), 1)
    sub = lax.broadcasted_iota(jnp.int32, (8, NZ * ROWS), 0)
    chosen = []
    for j in range(2):
        for c in range(0, PLANE, 2):
            place = jnp.full((8, NZ * ROWS), -1, jnp.int32)
            for row in range(8):
                if row % 4 < KBD:
                    block = own_ref[z * PKB + (c + row // 4) * KBD + row % 4]
                    lane = block // PKB * ROWS + j * PKB + lax.rem(block, PKB)
                    place = jnp.where(sub == row, lane, place)
            chosen.append(jnp.where(wide == place, 1.0, 0.0))
    chosen = jnp.concatenate(chosen, axis=0)
    for r in range(1, NZ):
        pr_copy(r).wait_send()
        tp_copy(r).wait_send()
    for c in range(CHUNKS):
        ring_copy(2 * c // CHUNKS, HALF, c).wait_send()
    for r in range(1, NZ):
        ms_arrival(r).wait_recv()
    spread = jnp.concatenate(
        [jnp.where(sub == 0, jnp.broadcast_to(mass_in[piece], (8, NZ * ROWS)), 0.0) for piece in range(NZ)], axis=0
    )
    rows = lax.dot_general(
        chosen, spread, (((1,), (1,)), ((), ())),
        precision=lax.Precision.HIGHEST, preferred_element_type=jnp.float32,
    )
    rows = pltpu.roll(rows[0:16] + pltpu.roll(rows[16:32], 1, 1), 2 * cls, 1)
    for c in range(PLANE):
        plane_out[c] = rows[4 * c:4 * c + 4]
    plane_in[cls] = plane_out[cls]

    def pe_copy(i):
        other = lax.rem(cls + i, PLANE)
        return remote(plane_out.at[other], plane_in.at[cls], pe_send.at[i], pe_recv.at[i], at_plane(cls + i))

    def pe_arrival(i):
        other = lax.rem(cls - i + PLANE, PLANE)
        return remote(plane_out.at[other], plane_in.at[other], pe_send.at[i], pe_recv.at[i], at_plane(cls - i))

    for i in range(1, PLANE):
        pe_copy(i).start()
    for r in range(1, NZ):
        ms_copy(r).wait_send()
    for i in range(1, PLANE):
        pe_arrival(i).wait_recv()
    final = plane_in[0] + plane_in[1] + plane_in[2] + plane_in[3]
    o_ref[0] = final[0:KBD]
    for i in range(1, PLANE):
        pe_copy(i).wait_send()


def body(queries, keys, head_pick, block_offset, owner_map):
    vmem = pl.BlockSpec(memory_space=pltpu.VMEM)
    smem = pl.BlockSpec(memory_space=pltpu.SMEM)
    hbm = pl.BlockSpec(memory_space=pl.ANY)
    f32, bf16 = jnp.float32, jnp.bfloat16
    dma = pltpu.SemaphoreType.DMA
    return pl.pallas_call(
        kernel,
        out_shape=jax.ShapeDtypeStruct((1, KBD, BLK), f32),
        in_specs=[hbm, hbm, smem, smem, smem],
        out_specs=vmem,
        scratch_shapes=[
            pltpu.VMEM((NZ, Q_DEV, HD), bf16),
            pltpu.VMEM((PLANE * K_DEV, HD), bf16),
            pltpu.VMEM((16, HD), bf16),
            pltpu.VMEM((NH, 16, HD), bf16),
            pltpu.VMEM((NH, PIECE, HD), bf16),
            pltpu.VMEM((NH, PIECE, HD), bf16),
            pltpu.VMEM((3, BLK, BLK), f32),
            pltpu.VMEM((NZ, ROWS, BLK), f32),
            pltpu.VMEM((NZ, 2, BLK), f32),
            pltpu.VMEM((ROWS, BLK), f32),
            pltpu.VMEM((NZ, ROWS, BLK), f32),
            pltpu.VMEM((NZ, 2, BLK), f32),
            pltpu.VMEM((NZ * ROWS, BLK), f32),
            pltpu.VMEM((1, NZ * ROWS), f32),
            pltpu.VMEM((NZ, 1, NZ * ROWS), f32),
            pltpu.VMEM((PLANE, 4, BLK), f32),
            pltpu.VMEM((PLANE, 4, BLK), f32),
            dma((2,)), pltpu.SemaphoreType.REGULAR((3, 2)),
            dma((2, HALF, CHUNKS)), dma((2, HALF, CHUNKS)),
            dma((NH,)), dma((NH,)),
            dma((NH,)), dma((NH,)),
            dma((NH, 2)), dma((NH, 2)),
            dma((2,)), dma((2,)),
            dma((NZ,)), dma((NZ,)),
            dma((NZ,)), dma((NZ,)),
            dma((NZ,)), dma((NZ,)),
            dma((PLANE,)), dma((PLANE,)),
        ],
        compiler_params=pltpu.CompilerParams(
            collective_id=0, has_side_effects=True, vmem_limit_bytes=60 * 1024 * 1024
        ),
        cost_estimate=pl.CostEstimate(flops=1610612736, bytes_accessed=165000, transcendentals=6291456),
    )(queries[0], keys[0], head_pick, block_offset, owner_map)


def solution(mesh):
    return jax.shard_map(
        body,
        mesh=mesh,
        in_specs=(P("head", "seq", None), P("head", "seq", None), P("head"), P("head"), P()),
        out_specs=P("head", "seq", None),
        check_vma=False,
    )
```

time: 291 us -> 64.5 us (0.22)
  waiting for transfers between devices: 134 us -> 0 us
  Pallas kernels: 0 us -> 61.7 us
  blocking collectives: 55.3 us -> 0 us
  matrix products: 42.9 us -> 0 us
  local copies, waits for them, and re-layouts: 19.7 us -> 1.25 us
  loops' own time: 15.6 us -> 0 us
  between operations: 14.8 us -> 1.3 us
  other arithmetic: 8.08 us -> 0 us
    all_gather x1 -> x0, waiting for transfers between devices: 134 us -> none  [body(): lax.all_gather(chosen, 'seq', axis=0, tiled=True)]
    pallas_call x0 -> x1, Pallas kernels: none -> 61.7 us  [body(): pl.pallas_call(kernel, out_shape=jax.ShapeDtypeStruct((1, KBD, BLK), f32)...]
    dot_general x24 -> x0, matrix products: 42.9 us -> none  [tile_scores(): lax.dot_general(query_rows, key_rows, (((1,), (1,)), ((), ())), preferred...]
    all_gather x1 -> x0, blocking collectives: 32.3 us -> none  [body(): every_head = lax.all_gather(keys, 'head', axis=0, tiled=True)]
    all_to_all x1 -> x0, blocking collectives: 23 us -> none  [body(): lax.all_to_all(ordered, 'seq', split_axis=0, concat_axis=1, tiled=True)]
    another operation x2 -> x0, loops' own time: 15.6 us -> none  [visit_tiles(): lax.scan(advance, carry, (jnp.arange(length // span, dtype=jnp.int32), ti...]
    dynamic_slice x25 -> x0, local copies, waits for them, and re-layouts: 14.8 us -> none  [the longest x24 14.2 us: visit_tiles(): lax.scan(advance, carry, (jnp.arange(length // span, dtype=jnp.int32), ti...]
    reduce_sum x13 -> x0, other arithmetic: 6.03 us -> none  [the longest x12 5.99 us: fold_stats(): jnp.sum(weights, axis=1)]
  transfers between devices with their start and end apart: 1 -> 0, of which waited for: 1 -> 0; matrix products, arithmetic and copies ran while one was open for 1% -> 0% of each run, Pallas kernels for 0% -> 0%
where the time goes in v2:
time: 64.5 us; the launch traced here: 64.3 us
  Pallas kernels  61.7 us (96%)
  between operations  1.3 us (2%)
  local copies, waits for them, and re-layouts  1.25 us (2%)
    pallas_call x1, Pallas kernels, body(): pl.pallas_call(kernel, out_shape=jax.ShapeDtypeStruct((1, KBD, BLK), f32)...  61.7 us

profile of v2, /device:TPU:1, one launch (start us, length us, event | category | flops | bytes accessed | tf_op | source)
XLA Modules:
  0.0 64.3 jit_solution(2327391067355372845)
XLA Ops:
  1.3 61.7 %shard_map.55 = f32[1,3,128]{2,1,0:T(4,128)} custom-call(bf16[256,128]{1,0:T(8,128)(2,1)} %bitcast.3, bf16[384,128]{1,0:T(8,128)(2,1)} %bitcast.2, s32[1]{0:T(128)S(6)} %copy.7.pick_ref, s32[1]{0:T(128)S(6)} %copy.8.off_ref, s32[192]{0:T(256)} %own_ref.1), custom_call_target="tpu_custom_call" | custom-call | flops 1610612736 | bytes 165000 | tf_op jit(solution)/shard_map/pallas_call | solution.py:381
  63.0 1.2 %copy.6 = f32[1,3,128]{2,0,1:T(1,128)} copy(f32[1,3,128]{2,1,0:T(4,128)} %shard_map.55) | data formatting | bytes 3072 | tf_op jit(solution)/shard_map/pallas_call | solution.py:381

commit v3 on v2

--- a/solution.py
+++ b/solution.py
@@ -21,7 +21,7 @@
 HALF = NZ // 2
 CHUNKS = 4
 CHUNK = Q_DEV // CHUNKS
-FIRST = 5
+EARLY = 5
 NEGATIVE = -1e30
 SCALE2 = 1.4426950408889634 * HD**-0.5
 MESH = pl.DeviceIdType.MESH
@@ -29,9 +29,9 @@
 
 def kernel(
     q_ref, k_ref, pick_ref, off_ref, own_ref, o_ref,
-    qall, kp, pick_out, picks, recv1, stage2, table, probs, tops, maxes, prob_in, top_in, weighted,
+    qall, kp, pick_out, picks, recv1, stage2, table, probs, tops, raw, maxes, prob_in, top_in, weighted,
     mass_out, mass_in, plane_out, plane_in,
-    local_sem, greet, ring_send, ring_recv, pk_send, pk_recv, s1_send, s1_recv, s2_send, s2_recv, s3_send, s3_recv,
+    local_sem, greet, ring_send, ring_recv, leaf_send, leaf_recv, pk_send, pk_recv, s1_send, s1_recv, s2_send, s2_recv, s3_send, s3_recv,
     pr_send, pr_recv, tp_send, tp_recv, ms_send, ms_recv, pe_send, pe_recv,
 ):
     head = lax.axis_index("head")
@@ -67,7 +67,7 @@
 
     barrier = pltpu.get_barrier_semaphore()
     s2_pairs = [(gi, xo) for gi in range(NH) for xo in range(2) if gi or xo]
-    near = [at_z(z + 1), at_z(z - 1)]
+    near = [at_z(z + 1), at_z(z - 1), at_z(z + 2), at_z(z - 2)]
     near += [at_pair(gi, xo) for gi, xo in s2_pairs]
     near += [{"head": head, "seq": z * PLANE + lax.rem(xl + xo, 2) * 2 + (1 - core)} for xo in range(2)]
     for device in near:
@@ -83,39 +83,68 @@
 
     pl.semaphore_wait(barrier, len(near))
 
-    def ring_copy(direction, d, c, src=None):
-        sign = 1 - 2 * direction
-        ref = qall.at[wrap(z - sign * (d - 1)), pl.ds(c * CHUNK, CHUNK), :]
-        return remote(
-            ref if src is None else src, ref,
-            ring_send.at[direction, d - 1, c], ring_recv.at[direction, d - 1, c], at_z(z + sign),
-        )
-
-    def ring_arrival(direction, d, c):
-        sign = 1 - 2 * direction
-        ref = qall.at[wrap(z - sign * d), pl.ds(c * CHUNK, CHUNK), :]
-        return remote(
-            ref, ref, ring_send.at[direction, d - 1, c], ring_recv.at[direction, d - 1, c], at_z(z + sign)
-        )
-
-    def first_ring_copy(direction, c):
-        return ring_copy(direction, 1, c, q_ref.at[pl.ds(c * CHUNK, CHUNK), :])
+    def sign_of(direction):
+        return 1 - 2 * direction
+
+    def chunk_rows(c):
+        return pl.ds(c * CHUNK, CHUNK)
+
+    def trunk_copy(direction, d, c):
+        sign = sign_of(direction)
+        ref = qall.at[wrap(z - sign * (d - 2)), chunk_rows(c), :]
+        return remote(
+            q_ref.at[chunk_rows(c), :] if d == 2 else ref, ref,
+            ring_send.at[direction, d // 2 - 1, c], ring_recv.at[direction, d // 2 - 1, c], at_z(z + 2 * sign),
+        )
+
+    def trunk_arrival(direction, d, c):
+        sign = sign_of(direction)
+        ref = qall.at[wrap(z - sign * d), chunk_rows(c), :]
+        return remote(
+            ref, ref,
+            ring_send.at[direction, d // 2 - 1, c], ring_recv.at[direction, d // 2 - 1, c], at_z(z - 2 * sign),
+        )
+
+    def leaf_copy(direction, d):
+        sign = sign_of(direction)
+        ref = qall.at[wrap(z - sign * (d - 1))]
+        return remote(
+            q_ref if d == 1 else ref, ref,
+            leaf_send.at[direction, d // 2], leaf_recv.at[direction, d // 2], at_z(z + sign),
+        )
+
+    def leaf_arrival(direction, d):
+        sign = sign_of(direction)
+        ref = qall.at[wrap(z - sign * d)]
+        return remote(
+            ref, ref, leaf_send.at[direction, d // 2], leaf_recv.at[direction, d // 2], at_z(z - sign)
+        )
 
     def serve(d, c):
         for direction in range(2):
-            ring_arrival(direction, d, c).wait_recv()
-            if isinstance(d, int):
-                ring_copy(direction, d + 1, c).start()
+            trunk_arrival(direction, d, c).wait_recv()
+            if d + 2 < HALF:
+                trunk_copy(direction, d + 2, c).start()
+            elif isinstance(c, int):
+                if c * 2 // CHUNKS == direction:
+                    trunk_copy(direction, d + 2, c).start()
             else:
-                mine = c < CHUNKS // 2 if direction == 0 else c >= CHUNKS // 2
-
-                @pl.when(jnp.logical_or(d < HALF - 1, mine))
+                @pl.when(c * 2 // CHUNKS == direction)
                 def _():
-                    ring_copy(direction, d + 1, c).start()
-
-    def ring_step(d):
+                    trunk_copy(direction, d + 2, c).start()
+
+    def serve_leaves(d):
+        for direction in range(2):
+            leaf_copy(direction, d).start()
+
+    def trunk_step(d):
         for c in range(CHUNKS):
             serve(d, c)
+        serve_leaves(d + 1)
+
+    def wait_leaves(d):
+        for direction in range(2):
+            leaf_arrival(direction, d).wait_recv()
 
     def s1_copy(i):
         other = lax.rem(head + i, NH)
@@ -139,33 +168,35 @@
     def s2_copy(gi, xo):
         other = lax.rem(head + gi, NH)
         return remote(
-            stage2.at[other], kp.at[pl.ds(cls * K_DEV + head * PIECE, PIECE), :],
+            stage2.at[other], kp.at[pl.ds(xl * K_DEV + head * PIECE, PIECE), :],
             s2_send.at[gi, xo], s2_recv.at[gi, xo], at_pair(gi, xo),
         )
 
     def s2_arrival(gi, xo):
         other = lax.rem(head - gi + NH, NH)
-        start = (lax.rem(xl + xo, 2) * 2 + core) * K_DEV + other * PIECE
+        start = lax.rem(xl + xo, 2) * K_DEV + other * PIECE
         return remote(
             stage2.at[other], kp.at[pl.ds(start, PIECE), :],
             s2_send.at[gi, xo], s2_recv.at[gi, xo], at_pair(-gi, xo),
         )
 
-    def s3_copy(xo, c):
-        ref = kp.at[pl.ds((2 * xo + c) * K_DEV, K_DEV), :]
-        return remote(
-            ref, ref, s3_send.at[xo], s3_recv.at[xo], {"head": head, "seq": z * PLANE + xl * 2 + (1 - core)}
-        )
-
-    for i in range(1, NH):
-        pk_copy(i).start()
-    for c in range(CHUNKS):
-        for direction in range(2):
-            first_ring_copy(direction, c).start()
+    def s3_copy():
+        return remote(
+            kp.at[pl.ds(0, 2 * K_DEV), :], kp.at[pl.ds(2 * K_DEV, 2 * K_DEV), :], s3_send.at[0], s3_recv.at[0],
+            {"head": head, "seq": z * PLANE + xl * 2 + (1 - core)},
+        )
+
+    for direction in range(2):
+        trunk_copy(direction, 2, 0).start()
     for i in range(1, NH):
         s1_copy(i).start()
+        pk_copy(i).start()
+    for c in range(1, CHUNKS):
+        for direction in range(2):
+            trunk_copy(direction, 2, c).start()
+    serve_leaves(1)
     for side in range(2):
-        signal(greet.at[0, side], at_z(z + 1 - 2 * side))
+        signal(greet.at[0, side], at_z(z + 2 - 4 * side))
 
     key_local = lax.broadcasted_iota(jnp.int32, (BLK, BLK), 0)
     query_local = lax.broadcasted_iota(jnp.int32, (BLK, BLK), 1)
@@ -173,11 +204,11 @@
     table[1] = jnp.where(key_local <= query_local, 0.0, NEGATIVE)
     table[2] = jnp.zeros((BLK, BLK), jnp.float32)
 
-    ring_step(1)
+    trunk_step(2)
     for side in range(2):
         pl.semaphore_wait(greet.at[0, side], 1)
     for side in range(2):
-        signal(greet.at[1, side], at_z(z + 2 - 4 * side))
+        signal(greet.at[1, side], at_z(z + 4 - 8 * side))
     own_k.wait()
     for i in range(1, NH):
         pk_arrival(i).wait_recv()
@@ -192,23 +223,15 @@
         stage2[g] = chosen.astype(jnp.bfloat16)
     for gi, xo in s2_pairs:
         s2_copy(gi, xo).start()
-    kp[pl.ds(cls * K_DEV + head * PIECE, PIECE), :] = stage2[head]
-    ring_step(2)
+    kp[pl.ds(xl * K_DEV + head * PIECE, PIECE), :] = stage2[head]
+    trunk_step(4)
     for side in range(2):
         pl.semaphore_wait(greet.at[1, side], 1)
-    for side in range(2):
-        signal(greet.at[2, side], at_z(z + 4 - 8 * side))
-    ring_step(3)
+    wait_leaves(1)
+    own_q.wait()
     for gi, xo in s2_pairs:
         s2_arrival(gi, xo).wait_recv()
-    for xo in range(2):
-        s3_copy(xo, core).start()
-    ring_step(4)
-    for side in range(2):
-        pl.semaphore_wait(greet.at[2, side], 1)
-    for xo in range(2):
-        s3_copy(xo, 1 - core).wait_recv()
-    own_q.wait()
+    s3_copy().start()
 
     offset = off_ref[0]
     far = wrap(z + HALF)
@@ -227,72 +250,112 @@
         source = wrap(z - r)
         return remote(tops.at[source], top_in.at[source], tp_send.at[r], tp_recv.at[r], at_z(z - r))
 
-    def compute(item, unused):
-        later = HALF * 2 - CHUNKS
-
-        @pl.when(item < later)
-        def _():
-            serve(FIRST + item // CHUNKS, lax.rem(item, CHUNKS))
-
-        @pl.when(item == 2 * HALF - 1)
-        def _():
-            for c in range(CHUNKS):
-                ring_arrival(2 * c // CHUNKS, HALF, c).wait_recv()
-
+    first = lax.broadcasted_iota(jnp.int32, (ROWS, BLK), 0) < PKB
+
+    def signed_of(item):
         d = (item + 1) // 2
-        signed = jnp.where(lax.rem(item, 2) == 1, -d, d)
-        slot = wrap(z + signed)
+        return jnp.where(lax.rem(item, 2) == 1, -d, d)
+
+    def scores(item, lo, hi):
+        slot = wrap(z + signed_of(item))
         q = qall[slot]
-        for kb in range(PKB):
+        for kb in range(lo, hi):
             s = lax.dot_general(
                 kp[kb * BLK:(kb + 1) * BLK, :], q, (((1,), (1,)), ((), ())),
                 preferred_element_type=jnp.float32,
             )
+            owner_core = core if kb < PKB // 2 else 1 - core
+            place = z * PKB + (kb // KBD % 2 * 2 + owner_core) * KBD + kb % KBD
             for j in range(2):
-                ahead = slot * 8 + cls * 2 + j + offset - (z * PKB + kb)
+                ahead = slot * 8 + cls * 2 + j + offset - place
                 sj = s[:, j * BLK:(j + 1) * BLK] + table[jnp.clip(ahead + 1, 0, 2)]
                 top = jnp.max(sj, axis=0, keepdims=True)
                 row = j * PKB + kb
-                maxes[row:row + 1, :] = top
-                probs[slot, row:row + 1, :] = jnp.sum(jnp.exp2((sj - top) * SCALE2), axis=0, keepdims=True)
-        first = lax.broadcasted_iota(jnp.int32, (ROWS, BLK), 0) < PKB
-        every = maxes[...]
+                maxes[item, row:row + 1, :] = top
+                raw[item, row:row + 1, :] = jnp.sum(jnp.exp2((sj - top) * SCALE2), axis=0, keepdims=True)
+
+    def close(item):
+        slot = wrap(z + signed_of(item))
+        every = maxes[item]
         top0 = jnp.max(jnp.where(first, every, NEGATIVE), axis=0, keepdims=True)
         top1 = jnp.max(jnp.where(first, NEGATIVE, every), axis=0, keepdims=True)
         tops[slot, 0:1, :] = top0
         tops[slot, 1:2, :] = top1
-        probs[slot] = probs[slot] * jnp.exp2((every - jnp.where(first, top0, top1)) * SCALE2)
-        r = HALF + signed
-
-        @pl.when(item < 2 * HALF - 1)
-        def _():
-            pr_copy(r).start()
-            tp_copy(r).start()
-
+        probs[slot] = raw[item] * jnp.exp2((every - jnp.where(first, top0, top1)) * SCALE2)
+
+    def send_sums(item):
+        r = HALF + signed_of(item)
+        pr_copy(r).start()
+        tp_copy(r).start()
+
+    def early(item, unused):
+        scores(item, 0, PKB // 2)
         return unused
 
-    lax.fori_loop(0, 2 * HALF, compute, 0)
+    def middle(item, unused):
+        @pl.when(item >= 1)
+        def _():
+            serve(6, item - 1)
+
+        close(jnp.maximum(item - 1, 0))
+        scores(item, PKB // 2, PKB)
+
+        @pl.when(item >= 1)
+        def _():
+            send_sums(item - 1)
+
+        return unused
+
+    def late(item, unused):
+        @pl.when(item == EARLY)
+        def _():
+            serve_leaves(7)
+            wait_leaves(3)
+
+        @pl.when(item == 9)
+        def _():
+            wait_leaves(5)
+
+        @pl.when(item == 13)
+        def _():
+            wait_leaves(7)
+
+        @pl.when(item == 15)
+        def _():
+            for c in range(CHUNKS):
+                trunk_arrival(c * 2 // CHUNKS, HALF, c).wait_recv()
+
+        close(item - 1)
+        scores(item, 0, PKB)
+        send_sums(item - 1)
+        return unused
+
+    lax.fori_loop(0, EARLY, early, 0)
+    s3_copy().wait_recv()
+    lax.fori_loop(0, EARLY, middle, 0)
+    lax.fori_loop(EARLY, 2 * HALF, late, 0)
+    close(2 * HALF - 1)
 
     prob_in[z] = probs[far]
     top_in[z] = tops[far]
     for direction in range(2):
-        for d in range(1, HALF):
+        for d in range(2, HALF, 2):
             for c in range(CHUNKS):
-                (first_ring_copy(direction, c) if d == 1 else ring_copy(direction, d, c)).wait_send()
+                trunk_copy(direction, d, c).wait_send()
+        for d in range(1, HALF, 2):
+            leaf_copy(direction, d).wait_send()
     for i in range(1, NH):
         pk_copy(i).wait_send()
         s1_copy(i).wait_send()
     for gi, xo in s2_pairs:
         s2_copy(gi, xo).wait_send()
-    for xo in range(2):
-        s3_copy(xo, core).wait_send()
+    s3_copy().wait_send()
     for r in range(1, NZ):
         tp_arrival(r).wait_recv()
         pr_arrival(r).wait_recv()
     each = top_in[...]
     top = jnp.max(each, axis=0, keepdims=True)
     factor = jnp.exp2((each - top) * SCALE2)
-    first = lax.broadcasted_iota(jnp.int32, (ROWS, BLK), 0) < PKB
     total = jnp.zeros((ROWS, BLK), jnp.float32)
     for source in range(NZ):
         part = prob_in[source] * jnp.where(first, factor[source, 0:1], factor[source, 1:2])
@@ -329,7 +392,10 @@
             for row in range(8):
                 if row % 4 < KBD:
                     block = own_ref[z * PKB + (c + row // 4) * KBD + row % 4]
-                    lane = block // PKB * ROWS + j * PKB + lax.rem(block, PKB)
+                    device = lax.rem(block, PKB) // KBD
+                    other_core = lax.rem(device + core, 2)
+                    inner = (other_core * 2 + device // 2) * KBD + lax.rem(block, KBD)
+                    lane = block // PKB * ROWS + j * PKB + inner
                     place = jnp.where(sub == row, lane, place)
             chosen.append(jnp.where(wide == place, 1.0, 0.0))
     chosen = jnp.concatenate(chosen, axis=0)
@@ -337,7 +403,7 @@
         pr_copy(r).wait_send()
         tp_copy(r).wait_send()
     for c in range(CHUNKS):
-        ring_copy(2 * c // CHUNKS, HALF, c).wait_send()
+        trunk_copy(c * 2 // CHUNKS, HALF, c).wait_send()
     for r in range(1, NZ):
         ms_arrival(r).wait_recv()
     spread = jnp.concatenate(
@@ -393,7 +459,8 @@
             pltpu.VMEM((3, BLK, BLK), f32),
             pltpu.VMEM((NZ, ROWS, BLK), f32),
             pltpu.VMEM((NZ, 2, BLK), f32),
-            pltpu.VMEM((ROWS, BLK), f32),
+            pltpu.VMEM((NZ, ROWS, BLK), f32),
+            pltpu.VMEM((NZ, ROWS, BLK), f32),
             pltpu.VMEM((NZ, ROWS, BLK), f32),
             pltpu.VMEM((NZ, 2, BLK), f32),
             pltpu.VMEM((NZ * ROWS, BLK), f32),
@@ -401,12 +468,13 @@
             pltpu.VMEM((NZ, 1, NZ * ROWS), f32),
             pltpu.VMEM((PLANE, 4, BLK), f32),
             pltpu.VMEM((PLANE, 4, BLK), f32),
-            dma((2,)), pltpu.SemaphoreType.REGULAR((3, 2)),
-            dma((2, HALF, CHUNKS)), dma((2, HALF, CHUNKS)),
+            dma((2,)), pltpu.SemaphoreType.REGULAR((2, 2)),
+            dma((2, HALF // 2, CHUNKS)), dma((2, HALF // 2, CHUNKS)),
+            dma((2, HALF // 2)), dma((2, HALF // 2)),
             dma((NH,)), dma((NH,)),
             dma((NH,)), dma((NH,)),
             dma((NH, 2)), dma((NH, 2)),
-            dma((2,)), dma((2,)),
+            dma((1,)), dma((1,)),
             dma((NZ,)), dma((NZ,)),
             dma((NZ,)), dma((NZ,)),
             dma((NZ,)), dma((NZ,)),

time: 64.5 us -> 61.3 us (0.950)
  Pallas kernels: 61.7 us -> 58.6 us
    pallas_call x1, Pallas kernels: 61.7 us -> 58.6 us  [body(): pl.pallas_call(kernel, out_shape=jax.ShapeDtypeStruct((1, KBD, BLK), f32)...]
where the time goes in v3:
time: 61.3 us; the launch traced here: 61.1 us
  Pallas kernels  58.6 us (96%)
  between operations  1.3 us (2%)
  local copies, waits for them, and re-layouts  1.25 us (2%)
    pallas_call x1, Pallas kernels, body(): pl.pallas_call(kernel, out_shape=jax.ShapeDtypeStruct((1, KBD, BLK), f32)...  58.6 us
    pallas_call x1, local copies, waits for them, and re-layouts, body(): pl.pallas_call(kernel, out_shape=jax.ShapeDtypeStruct((1, KBD, BLK), f32)...  1.25 us

profile of v3, /device:TPU:1, one launch (start us, length us, event | category | flops | bytes accessed | tf_op | source)
XLA Modules:
  0.0 61.1 jit_solution(6120547797989973490)
XLA Ops:
  1.3 58.6 %shard_map.55 = f32[1,3,128]{2,1,0:T(4,128)} custom-call(bf16[256,128]{1,0:T(8,128)(2,1)} %bitcast.3, bf16[384,128]{1,0:T(8,128)(2,1)} %bitcast.2, s32[1]{0:T(128)S(6)} %copy.7.pick_ref, s32[1]{0:T(128)S(6)} %copy.8.off_ref, s32[192]{0:T(256)} %own_ref.1), custom_call_target="tpu_custom_call" | custom-call | flops 1610612736 | bytes 165000 | tf_op jit(solution)/shard_map/pallas_call | solution.py:447
  59.9 1.2 %copy.6 = f32[1,3,128]{2,0,1:T(1,128)} copy(f32[1,3,128]{2,1,0:T(4,128)} %shard_map.55) | data formatting | bytes 3072 | tf_op jit(solution)/shard_map/pallas_call | solution.py:447

commit v4 on v3

--- a/solution.py
+++ b/solution.py
@@ -19,19 +19,21 @@
 PKB = PLANE * KBD
 ROWS = 2 * PKB
 HALF = NZ // 2
-CHUNKS = 4
+CHUNKS = 2
 CHUNK = Q_DEV // CHUNKS
 EARLY = 5
+QBD = Q_DEV // BLK * PLANE
+REACH = 64 + QBD - 1
 NEGATIVE = -1e30
 SCALE2 = 1.4426950408889634 * HD**-0.5
 MESH = pl.DeviceIdType.MESH
 
 
 def kernel(
-    q_ref, k_ref, pick_ref, off_ref, own_ref, o_ref,
+    q_ref, k_ref, pick_hbm, off_hbm, own_hbm, o_ref,
     qall, kp, pick_out, picks, recv1, stage2, table, probs, tops, raw, maxes, prob_in, top_in, weighted,
     mass_out, mass_in, plane_out, plane_in,
-    local_sem, greet, ring_send, ring_recv, leaf_send, leaf_recv, pk_send, pk_recv, s1_send, s1_recv, s2_send, s2_recv, s3_send, s3_recv,
+    pick_ref, off_ref, own_ref, local_sem, greet, ring_send, ring_recv, leaf_send, leaf_recv, pk_send, pk_recv, s1_send, s1_recv, s2_send, s2_recv, s3_send, s3_recv,
     pr_send, pr_recv, tp_send, tp_recv, ms_send, ms_recv, pe_send, pe_recv,
 ):
     head = lax.axis_index("head")
@@ -75,11 +77,15 @@
 
     own_q = pltpu.make_async_copy(q_ref, qall.at[z], local_sem.at[0])
     own_k = pltpu.make_async_copy(k_ref.at[pl.ds(head * PIECE, PIECE), :], recv1.at[head], local_sem.at[1])
+    scalars = [
+        pltpu.make_async_copy(pick_hbm, pick_ref, local_sem.at[2]),
+        pltpu.make_async_copy(off_hbm, off_ref, local_sem.at[3]),
+        pltpu.make_async_copy(own_hbm, own_ref, local_sem.at[4]),
+    ]
+    for copy in scalars:
+        copy.start()
+    own_k.start()
     own_q.start()
-    own_k.start()
-    picked = (pick_ref[0] // (QH // KV)).astype(jnp.float32)
-    pick_out[...] = jnp.full((16, HD), picked, jnp.float32).astype(jnp.bfloat16)
-    picks[head] = pick_out[...]
 
     pl.semaphore_wait(barrier, len(near))
 
@@ -120,22 +126,34 @@
             ref, ref, leaf_send.at[direction, d // 2], leaf_recv.at[direction, d // 2], at_z(z - sign)
         )
 
+    def meets(query_plane, key_plane):
+        return PKB * key_plane <= QBD * query_plane + REACH
+
+    def comes(direction, d, query_plane):
+        if direction == 1:
+            return query_plane >= d
+        if d % 2 == 0:
+            return jnp.logical_or(query_plane >= HALF, meets(query_plane, query_plane + d))
+        return jnp.logical_or(query_plane + d >= NZ, meets(query_plane, query_plane + d))
+
+    def when(condition, action):
+        @pl.when(condition)
+        def _():
+            action()
+
     def serve(d, c):
         for direction in range(2):
-            trunk_arrival(direction, d, c).wait_recv()
-            if d + 2 < HALF:
-                trunk_copy(direction, d + 2, c).start()
-            elif isinstance(c, int):
-                if c * 2 // CHUNKS == direction:
-                    trunk_copy(direction, d + 2, c).start()
-            else:
-                @pl.when(c * 2 // CHUNKS == direction)
-                def _():
-                    trunk_copy(direction, d + 2, c).start()
+            piece = wrap(z - sign_of(direction) * d)
+            goes_on = comes(direction, d + 2, piece)
+            if d + 2 == HALF:
+                goes_on = jnp.logical_and(goes_on, c * 2 // CHUNKS == direction)
+            when(comes(direction, d, piece), trunk_arrival(direction, d, c).wait_recv)
+            when(goes_on, trunk_copy(direction, d + 2, c).start)
 
     def serve_leaves(d):
         for direction in range(2):
-            leaf_copy(direction, d).start()
+            piece = wrap(z - sign_of(direction) * (d - 1))
+            when(comes(direction, d, piece), leaf_copy(direction, d).start)
 
     def trunk_step(d):
         for c in range(CHUNKS):
@@ -144,7 +162,8 @@
 
     def wait_leaves(d):
         for direction in range(2):
-            leaf_arrival(direction, d).wait_recv()
+            piece = wrap(z - sign_of(direction) * d)
+            when(comes(direction, d, piece), leaf_arrival(direction, d).wait_recv)
 
     def s1_copy(i):
         other = lax.rem(head + i, NH)
@@ -187,14 +206,20 @@
         )
 
     for direction in range(2):
-        trunk_copy(direction, 2, 0).start()
+        when(comes(direction, 2, z), trunk_copy(direction, 2, 0).start)
     for i in range(1, NH):
         s1_copy(i).start()
-        pk_copy(i).start()
     for c in range(1, CHUNKS):
         for direction in range(2):
-            trunk_copy(direction, 2, c).start()
+            when(comes(direction, 2, z), trunk_copy(direction, 2, c).start)
     serve_leaves(1)
+    for copy in scalars:
+        copy.wait()
+    picked = (pick_ref[0] // (QH // KV)).astype(jnp.float32)
+    pick_out[...] = jnp.full((16, HD), picked, jnp.float32).astype(jnp.bfloat16)
+    picks[head] = pick_out[...]
+    for i in range(1, NH):
+        pk_copy(i).start()
     for side in range(2):
         signal(greet.at[0, side], at_z(z + 2 - 4 * side))
 
@@ -274,8 +299,7 @@
                 maxes[item, row:row + 1, :] = top
                 raw[item, row:row + 1, :] = jnp.sum(jnp.exp2((sj - top) * SCALE2), axis=0, keepdims=True)
 
-    def close(item):
-        slot = wrap(z + signed_of(item))
+    def close(item, slot):
         every = maxes[item]
         top0 = jnp.max(jnp.where(first, every, NEGATIVE), axis=0, keepdims=True)
         top1 = jnp.max(jnp.where(first, NEGATIVE, every), axis=0, keepdims=True)
@@ -288,22 +312,32 @@
         pr_copy(r).start()
         tp_copy(r).start()
 
+    def wanted_item(item):
+        return meets(wrap(z + signed_of(item)), z)
+
     def early(item, unused):
-        scores(item, 0, PKB // 2)
+        when(wanted_item(item), lambda: scores(item, 0, PKB // 2))
         return unused
 
+    def slot_of(item):
+        return wrap(z + signed_of(item))
+
+    def step(item, lo, closed=False):
+        before = jnp.maximum(item - 1, 0)
+        now, ended = wanted_item(item), wanted_item(before)
+        ended = jnp.logical_and(ended, jnp.logical_not(closed))
+
+        @pl.when(now)
+        def _():
+            close(before, jnp.where(closed, NZ, slot_of(before)))
+            scores(item, lo, PKB)
+
+        when(jnp.logical_and(jnp.logical_not(now), ended), lambda: close(before, slot_of(before)))
+        when(jnp.logical_and(ended, item >= 1), lambda: send_sums(before))
+
     def middle(item, unused):
-        @pl.when(item >= 1)
-        def _():
-            serve(6, item - 1)
-
-        close(jnp.maximum(item - 1, 0))
-        scores(item, PKB // 2, PKB)
-
-        @pl.when(item >= 1)
-        def _():
-            send_sums(item - 1)
-
+        when(jnp.logical_and(item >= 1, item < 1 + CHUNKS), lambda: serve(6, item - 1))
+        step(item, PKB // 2)
         return unused
 
     def late(item, unused):
@@ -312,38 +346,51 @@
             serve_leaves(7)
             wait_leaves(3)
 
+        waits = jnp.logical_or(item == 9, jnp.logical_or(item == 13, item == 15))
+
+        @pl.when(jnp.logical_and(waits, wanted_item(item - 1)))
+        def _():
+            close(item - 1, slot_of(item - 1))
+            send_sums(item - 1)
+
         @pl.when(item == 9)
         def _():
             wait_leaves(5)
 
-        @pl.when(item == 13)
-        def _():
-            wait_leaves(7)
-
-        @pl.when(item == 15)
+        when(item == 13, lambda: wait_leaves(7))
+
+        @pl.when(jnp.logical_and(item == 15, far >= HALF))
         def _():
             for c in range(CHUNKS):
                 trunk_arrival(c * 2 // CHUNKS, HALF, c).wait_recv()
 
-        close(item - 1)
-        scores(item, 0, PKB)
-        send_sums(item - 1)
+        step(item, 0, waits)
         return unused
 
     lax.fori_loop(0, EARLY, early, 0)
     s3_copy().wait_recv()
     lax.fori_loop(0, EARLY, middle, 0)
     lax.fori_loop(EARLY, 2 * HALF, late, 0)
-    close(2 * HALF - 1)
-
-    prob_in[z] = probs[far]
-    top_in[z] = tops[far]
+
+    def no_sums(source):
+        prob_in[source] = jnp.zeros((ROWS, BLK), jnp.float32)
+        top_in[source] = jnp.full((2, BLK), NEGATIVE, jnp.float32)
+
+    @pl.when(meets(far, z))
+    def _():
+        close(2 * HALF - 1, far)
+        prob_in[z] = probs[far]
+        top_in[z] = tops[far]
+
+    when(jnp.logical_not(meets(far, z)), lambda: no_sums(z))
     for direction in range(2):
         for d in range(2, HALF, 2):
             for c in range(CHUNKS):
-                trunk_copy(direction, d, c).wait_send()
+                piece = wrap(z - sign_of(direction) * (d - 2))
+                when(comes(direction, d, piece), trunk_copy(direction, d, c).wait_send)
         for d in range(1, HALF, 2):
-            leaf_copy(direction, d).wait_send()
+            piece = wrap(z - sign_of(direction) * (d - 1))
+            when(comes(direction, d, piece), leaf_copy(direction, d).wait_send)
     for i in range(1, NH):
         pk_copy(i).wait_send()
         s1_copy(i).wait_send()
@@ -351,8 +398,15 @@
         s2_copy(gi, xo).wait_send()
     s3_copy().wait_send()
     for r in range(1, NZ):
-        tp_arrival(r).wait_recv()
-        pr_arrival(r).wait_recv()
+        source = wrap(z - r)
+        sent = meets(far, source)
+
+        @pl.when(sent)
+        def _():
+            tp_arrival(r).wait_recv()
+            pr_arrival(r).wait_recv()
+
+        when(jnp.logical_not(sent), lambda: no_sums(source))
     each = top_in[...]
     top = jnp.max(each, axis=0, keepdims=True)
     factor = jnp.exp2((each - top) * SCALE2)
@@ -400,10 +454,15 @@
             chosen.append(jnp.where(wide == place, 1.0, 0.0))
     chosen = jnp.concatenate(chosen, axis=0)
     for r in range(1, NZ):
-        pr_copy(r).wait_send()
-        tp_copy(r).wait_send()
+        @pl.when(meets(wrap(z + HALF + r), z))
+        def _():
+            pr_copy(r).wait_send()
+            tp_copy(r).wait_send()
+
     for c in range(CHUNKS):
-        trunk_copy(c * 2 // CHUNKS, HALF, c).wait_send()
+        direction = c * 2 // CHUNKS
+        piece = wrap(z - sign_of(direction) * (HALF - 2))
+        when(comes(direction, HALF, piece), trunk_copy(direction, HALF, c).wait_send)
     for r in range(1, NZ):
         ms_arrival(r).wait_recv()
     spread = jnp.concatenate(
@@ -440,14 +499,13 @@
 
 def body(queries, keys, head_pick, block_offset, owner_map):
     vmem = pl.BlockSpec(memory_space=pltpu.VMEM)
-    smem = pl.BlockSpec(memory_space=pltpu.SMEM)
     hbm = pl.BlockSpec(memory_space=pl.ANY)
     f32, bf16 = jnp.float32, jnp.bfloat16
     dma = pltpu.SemaphoreType.DMA
     return pl.pallas_call(
         kernel,
         out_shape=jax.ShapeDtypeStruct((1, KBD, BLK), f32),
-        in_specs=[hbm, hbm, smem, smem, smem],
+        in_specs=[hbm] * 5,
         out_specs=vmem,
         scratch_shapes=[
             pltpu.VMEM((NZ, Q_DEV, HD), bf16),
@@ -457,8 +515,8 @@
             pltpu.VMEM((NH, PIECE, HD), bf16),
             pltpu.VMEM((NH, PIECE, HD), bf16),
             pltpu.VMEM((3, BLK, BLK), f32),
-            pltpu.VMEM((NZ, ROWS, BLK), f32),
-            pltpu.VMEM((NZ, 2, BLK), f32),
+            pltpu.VMEM((NZ + 1, ROWS, BLK), f32),
+            pltpu.VMEM((NZ + 1, 2, BLK), f32),
             pltpu.VMEM((NZ, ROWS, BLK), f32),
             pltpu.VMEM((NZ, ROWS, BLK), f32),
             pltpu.VMEM((NZ, ROWS, BLK), f32),
@@ -468,7 +526,10 @@
             pltpu.VMEM((NZ, 1, NZ * ROWS), f32),
             pltpu.VMEM((PLANE, 4, BLK), f32),
             pltpu.VMEM((PLANE, 4, BLK), f32),
-            dma((2,)), pltpu.SemaphoreType.REGULAR((2, 2)),
+            pltpu.SMEM((1,), jnp.int32),
+            pltpu.SMEM((1,), jnp.int32),
+            pltpu.SMEM((NZ * PKB,), jnp.int32),
+            dma((5,)), pltpu.SemaphoreType.REGULAR((2, 2)),
             dma((2, HALF // 2, CHUNKS)), dma((2, HALF // 2, CHUNKS)),
             dma((2, HALF // 2)), dma((2, HALF // 2)),
             dma((NH,)), dma((NH,)),

time: 61.3 us -> 59.7 us (0.974)
  Pallas kernels: 58.6 us -> 57 us
    pallas_call x1, Pallas kernels: 58.6 us -> 57 us  [body(): pl.pallas_call(kernel, out_shape=jax.ShapeDtypeStruct((1, KBD, BLK), f32)...]
where the time goes in v4:
time: 59.7 us; the launch traced here: 59.5 us
  Pallas kernels  57 us (95%)
  between operations  1.3 us (2%)
  local copies, waits for them, and re-layouts  1.25 us (2%)
    pallas_call x1, Pallas kernels, body(): pl.pallas_call(kernel, out_shape=jax.ShapeDtypeStruct((1, KBD, BLK), f32)...  57 us
    pallas_call x1, local copies, waits for them, and re-layouts, body(): pl.pallas_call(kernel, out_shape=jax.ShapeDtypeStruct((1, KBD, BLK), f32)...  1.25 us

profile of v4, /device:TPU:1, one launch (start us, length us, event | category | flops | bytes accessed | tf_op | source)
XLA Modules:
  0.0 59.5 jit_solution(620707074621218169)
XLA Ops:
  1.3 57.0 %shard_map.55 = f32[1,3,128]{2,1,0:T(4,128)} custom-call(bf16[256,128]{1,0:T(8,128)(2,1)} %bitcast.3, bf16[384,128]{1,0:T(8,128)(2,1)} %bitcast.2, s32[1]{0:T(128)S(6)} %copy.7.pick_hbm, s32[1]{0:T(128)S(6)} %copy.8.off_hbm, s32[192]{0:T(256)} %own_hbm.1), custom_call_target="tpu_custom_call" | custom-call | flops 1610612736 | bytes 165000 | tf_op jit(solution)/shard_map/pallas_call | solution.py:505
  58.3 1.2 %copy.6 = f32[1,3,128]{2,0,1:T(1,128)} copy(f32[1,3,128]{2,1,0:T(4,128)} %shard_map.55) | data formatting | bytes 3072 | tf_op jit(solution)/shard_map/pallas_call | solution.py:505

commit v5 on v4

--- a/solution.py
+++ b/solution.py
@@ -22,6 +22,7 @@
 CHUNKS = 2
 CHUNK = Q_DEV // CHUNKS
 EARLY = 5
+FORWARD = 6
 QBD = Q_DEV // BLK * PLANE
 REACH = 64 + QBD - 1
 NEGATIVE = -1e30
@@ -254,6 +255,13 @@
         pl.semaphore_wait(greet.at[1, side], 1)
     wait_leaves(1)
     own_q.wait()
+
+    @pl.when(z >= FORWARD)
+    def _():
+        for c in range(CHUNKS):
+            serve(6, c)
+        serve_leaves(7)
+
     for gi, xo in s2_pairs:
         s2_arrival(gi, xo).wait_recv()
     s3_copy().start()
@@ -336,14 +344,15 @@
         when(jnp.logical_and(ended, item >= 1), lambda: send_sums(before))
 
     def middle(item, unused):
-        when(jnp.logical_and(item >= 1, item < 1 + CHUNKS), lambda: serve(6, item - 1))
+        serving = jnp.logical_and(item >= 1, item < 1 + CHUNKS)
+        when(jnp.logical_and(serving, z < FORWARD), lambda: serve(6, item - 1))
         step(item, PKB // 2)
         return unused
 
     def late(item, unused):
         @pl.when(item == EARLY)
         def _():
-            serve_leaves(7)
+            when(z < FORWARD, lambda: serve_leaves(7))
             wait_leaves(3)
 
         waits = jnp.logical_or(item == 9, jnp.logical_or(item == 13, item == 15))

time: 59.7 us -> 58.8 us (0.985)
  Pallas kernels: 57 us -> 56.1 us
    pallas_call x1, Pallas kernels: 57 us -> 56.1 us  [body(): pl.pallas_call(kernel, out_shape=jax.ShapeDtypeStruct((1, KBD, BLK), f32)...]
where the time goes in v5:
time: 58.8 us; the launch traced here: 58.7 us
  Pallas kernels  56.1 us (95%)
  between operations  1.3 us (2%)
  local copies, waits for them, and re-layouts  1.25 us (2%)
    pallas_call x1, Pallas kernels, body(): pl.pallas_call(kernel, out_shape=jax.ShapeDtypeStruct((1, KBD, BLK), f32)...  56.1 us
    pallas_call x1, local copies, waits for them, and re-layouts, body(): pl.pallas_call(kernel, out_shape=jax.ShapeDtypeStruct((1, KBD, BLK), f32)...  1.25 us

profile of v5, /device:TPU:1, one launch (start us, length us, event | category | flops | bytes accessed | tf_op | source)
XLA Modules:
  0.0 58.7 jit_solution(17814663969951931864)
XLA Ops:
  1.3 56.1 %shard_map.55 = f32[1,3,128]{2,1,0:T(4,128)} custom-call(bf16[256,128]{1,0:T(8,128)(2,1)} %bitcast.3, bf16[384,128]{1,0:T(8,128)(2,1)} %bitcast.2, s32[1]{0:T(128)S(6)} %copy.7.pick_hbm, s32[1]{0:T(128)S(6)} %copy.8.off_hbm, s32[192]{0:T(256)} %own_hbm.1), custom_call_target="tpu_custom_call" | custom-call | flops 1610612736 | bytes 165000 | tf_op jit(solution)/shard_map/pallas_call | solution.py:514
  57.4 1.2 %copy.6 = f32[1,3,128]{2,0,1:T(1,128)} copy(f32[1,3,128]{2,1,0:T(4,128)} %shard_map.55) | data formatting | bytes 3072 | tf_op jit(solution)/shard_map/pallas_call | solution.py:514

commit v6 on v5

--- a/solution.py
+++ b/solution.py
@@ -56,9 +56,6 @@
     def at_pair(gi, xo):
         return {"head": lax.rem(head + gi + NH, NH), "seq": z * PLANE + lax.rem(xl + xo, 2) * 2 + core}
 
-    def at_plane(c):
-        return {"head": head, "seq": z * PLANE + lax.rem(c + PLANE, PLANE)}
-
     def remote(src, dst, send, recv, device):
         return pltpu.make_async_remote_copy(
             src_ref=src, dst_ref=dst, send_sem=send, recv_sem=recv,
@@ -206,13 +203,11 @@
             {"head": head, "seq": z * PLANE + xl * 2 + (1 - core)},
         )
 
-    for direction in range(2):
-        when(comes(direction, 2, z), trunk_copy(direction, 2, 0).start)
+    for c in range(CHUNKS):
+        for direction in range(2):
+            when(comes(direction, 2, z), trunk_copy(direction, 2, c).start)
     for i in range(1, NH):
         s1_copy(i).start()
-    for c in range(1, CHUNKS):
-        for direction in range(2):
-            when(comes(direction, 2, z), trunk_copy(direction, 2, c).start)
     serve_leaves(1)
     for copy in scalars:
         copy.wait()
@@ -253,6 +248,7 @@
     trunk_step(4)
     for side in range(2):
         pl.semaphore_wait(greet.at[1, side], 1)
+    signal(greet.at[2, 0], at_pair(0, 1))
     wait_leaves(1)
     own_q.wait()
 
@@ -289,7 +285,7 @@
         d = (item + 1) // 2
         return jnp.where(lax.rem(item, 2) == 1, -d, d)
 
-    def scores(item, lo, hi):
+    def scores(item, lo, hi, masked=True):
         slot = wrap(z + signed_of(item))
         q = qall[slot]
         for kb in range(lo, hi):
@@ -301,7 +297,9 @@
             place = z * PKB + (kb // KBD % 2 * 2 + owner_core) * KBD + kb % KBD
             for j in range(2):
                 ahead = slot * 8 + cls * 2 + j + offset - place
-                sj = s[:, j * BLK:(j + 1) * BLK] + table[jnp.clip(ahead + 1, 0, 2)]
+                sj = s[:, j * BLK:(j + 1) * BLK]
+                if masked:
+                    sj = sj + table[jnp.clip(ahead + 1, 0, 2)]
                 top = jnp.max(sj, axis=0, keepdims=True)
                 row = j * PKB + kb
                 maxes[item, row:row + 1, :] = top
@@ -335,7 +333,14 @@
         now, ended = wanted_item(item), wanted_item(before)
         ended = jnp.logical_and(ended, jnp.logical_not(closed))
 
-        @pl.when(now)
+        whole = PKB * (z + 1) <= QBD * slot_of(item) + 2 * cls
+
+        @pl.when(jnp.logical_and(now, whole))
+        def _():
+            close(before, jnp.where(closed, NZ, slot_of(before)))
+            scores(item, lo, PKB, False)
+
+        @pl.when(jnp.logical_and(now, jnp.logical_not(whole)))
         def _():
             close(before, jnp.where(closed, NZ, slot_of(before)))
             scores(item, lo, PKB)
@@ -433,34 +438,37 @@
     )
     column = lax.broadcasted_iota(jnp.int32, (1, NZ * ROWS), 1)
     mass_out[...] = jnp.where(lax.rem(column, ROWS) < PKB, mass[0:1], mass[1:2])
-    mass_in[far] = mass_out[...]
-
-    def ms_copy(r):
-        return remote(mass_out, mass_in.at[far], ms_send.at[r], ms_recv.at[r], at_z(z + r))
-
-    def ms_arrival(r):
-        source = wrap(z - r + HALF)
-        return remote(mass_out, mass_in.at[source], ms_send.at[r], ms_recv.at[r], at_z(z - r))
-
-    for d in range(HALF):
-        ms_copy(HALF - d).start()
-        if d:
-            ms_copy(HALF + d).start()
+    mass_in[xl, far] = mass_out[...]
+
+    def at_line(xo, r):
+        return {"head": head, "seq": wrap(z + r) * PLANE + lax.rem(xl + xo, 2) * 2 + core}
+
+    def ms_copy(xo, r):
+        return remote(mass_out, mass_in.at[xl, far], ms_send.at[xo, r], ms_recv.at[xo, r], at_line(xo, r))
+
+    def ms_arrival(xo, r):
+        slot = mass_in.at[lax.rem(xl + xo, 2), wrap(z - r + HALF)]
+        return remote(mass_out, slot, ms_send.at[xo, r], ms_recv.at[xo, r], at_line(xo, -r))
+
+    crossings = [(xo, r) for d in range(HALF) for r in ((HALF - d, HALF + d) if d else (HALF,)) for xo in range(2)]
+    crossings.append((1, 0))
+    pl.semaphore_wait(greet.at[2, 0], 1)
+    for xo, r in crossings:
+        ms_copy(xo, r).start()
     wide = lax.broadcasted_iota(jnp.int32, (8, NZ * ROWS), 1)
     sub = lax.broadcasted_iota(jnp.int32, (8, NZ * ROWS), 0)
     chosen = []
     for j in range(2):
-        for c in range(0, PLANE, 2):
-            place = jnp.full((8, NZ * ROWS), -1, jnp.int32)
-            for row in range(8):
-                if row % 4 < KBD:
-                    block = own_ref[z * PKB + (c + row // 4) * KBD + row % 4]
-                    device = lax.rem(block, PKB) // KBD
-                    other_core = lax.rem(device + core, 2)
-                    inner = (other_core * 2 + device // 2) * KBD + lax.rem(block, KBD)
-                    lane = block // PKB * ROWS + j * PKB + inner
-                    place = jnp.where(sub == row, lane, place)
-            chosen.append(jnp.where(wide == place, 1.0, 0.0))
+        place = jnp.full((8, NZ * ROWS), -1, jnp.int32)
+        for row in range(8):
+            if row % 4 < KBD:
+                block = own_ref[z * PKB + (xl * 2 + row // 4) * KBD + row % 4]
+                device = lax.rem(block, PKB) // KBD
+                other_core = lax.rem(device + core, 2)
+                inner = (other_core * 2 + device // 2) * KBD + lax.rem(block, KBD)
+                lane = block // PKB * ROWS + j * PKB + inner
+                place = jnp.where(sub == row, lane, place)
+        chosen.append(jnp.where(wide == place, 1.0, 0.0))
     chosen = jnp.concatenate(chosen, axis=0)
     for r in range(1, NZ):
         @pl.when(meets(wrap(z + HALF + r), z))
@@ -472,38 +480,44 @@
         direction = c * 2 // CHUNKS
         piece = wrap(z - sign_of(direction) * (HALF - 2))
         when(comes(direction, HALF, piece), trunk_copy(direction, HALF, c).wait_send)
-    for r in range(1, NZ):
-        ms_arrival(r).wait_recv()
+    for xo, r in crossings:
+        ms_arrival(xo, r).wait_recv()
     spread = jnp.concatenate(
-        [jnp.where(sub == 0, jnp.broadcast_to(mass_in[piece], (8, NZ * ROWS)), 0.0) for piece in range(NZ)], axis=0
+        [
+            jnp.where(sub == 0, jnp.broadcast_to(mass_in[x, piece], (8, NZ * ROWS)), 0.0)
+            for x in range(2) for piece in range(NZ)
+        ],
+        axis=0,
     )
     rows = lax.dot_general(
         chosen, spread, (((1,), (1,)), ((), ())),
         precision=lax.Precision.HIGHEST, preferred_element_type=jnp.float32,
     )
-    rows = pltpu.roll(rows[0:16] + pltpu.roll(rows[16:32], 1, 1), 2 * cls, 1)
-    for c in range(PLANE):
+    rows = rows[0:8] + pltpu.roll(rows[8:16], 1, 1)
+    rows = pltpu.roll(rows[:, 0:BLK], 2 * core, 1) + pltpu.roll(rows[:, BLK:2 * BLK], 4 + 2 * core, 1)
+    for c in range(2):
         plane_out[c] = rows[4 * c:4 * c + 4]
-    plane_in[cls] = plane_out[cls]
-
-    def pe_copy(i):
-        other = lax.rem(cls + i, PLANE)
-        return remote(plane_out.at[other], plane_in.at[cls], pe_send.at[i], pe_recv.at[i], at_plane(cls + i))
-
-    def pe_arrival(i):
-        other = lax.rem(cls - i + PLANE, PLANE)
-        return remote(plane_out.at[other], plane_in.at[other], pe_send.at[i], pe_recv.at[i], at_plane(cls - i))
-
-    for i in range(1, PLANE):
-        pe_copy(i).start()
-    for r in range(1, NZ):
-        ms_copy(r).wait_send()
-    for i in range(1, PLANE):
-        pe_arrival(i).wait_recv()
-    final = plane_in[0] + plane_in[1] + plane_in[2] + plane_in[3]
+    plane_in[core] = plane_out[core]
+
+    def pe_copy():
+        return remote(
+            plane_out.at[1 - core], plane_in.at[core], pe_send.at[0], pe_recv.at[0],
+            {"head": head, "seq": z * PLANE + xl * 2 + (1 - core)},
+        )
+
+    def pe_arrival():
+        return remote(
+            plane_out.at[1 - core], plane_in.at[1 - core], pe_send.at[0], pe_recv.at[0],
+            {"head": head, "seq": z * PLANE + xl * 2 + (1 - core)},
+        )
+
+    pe_copy().start()
+    for xo, r in crossings:
+        ms_copy(xo, r).wait_send()
+    pe_arrival().wait_recv()
+    final = plane_in[0] + plane_in[1]
     o_ref[0] = final[0:KBD]
-    for i in range(1, PLANE):
-        pe_copy(i).wait_send()
+    pe_copy().wait_send()
 
 
 def body(queries, keys, head_pick, block_offset, owner_map):
@@ -532,13 +546,13 @@
             pltpu.VMEM((NZ, 2, BLK), f32),
             pltpu.VMEM((NZ * ROWS, BLK), f32),
             pltpu.VMEM((1, NZ * ROWS), f32),
-            pltpu.VMEM((NZ, 1, NZ * ROWS), f32),
-            pltpu.VMEM((PLANE, 4, BLK), f32),
-            pltpu.VMEM((PLANE, 4, BLK), f32),
+            pltpu.VMEM((2, NZ, 1, NZ * ROWS), f32),
+            pltpu.VMEM((2, 4, BLK), f32),
+            pltpu.VMEM((2, 4, BLK), f32),
             pltpu.SMEM((1,), jnp.int32),
             pltpu.SMEM((1,), jnp.int32),
             pltpu.SMEM((NZ * PKB,), jnp.int32),
-            dma((5,)), pltpu.SemaphoreType.REGULAR((2, 2)),
+            dma((5,)), pltpu.SemaphoreType.REGULAR((3, 2)),
             dma((2, HALF // 2, CHUNKS)), dma((2, HALF // 2, CHUNKS)),
             dma((2, HALF // 2)), dma((2, HALF // 2)),
             dma((NH,)), dma((NH,)),
@@ -547,8 +561,8 @@
             dma((1,)), dma((1,)),
             dma((NZ,)), dma((NZ,)),
             dma((NZ,)), dma((NZ,)),
-            dma((NZ,)), dma((NZ,)),
-            dma((PLANE,)), dma((PLANE,)),
+            dma((2, NZ)), dma((2, NZ)),
+            dma((1,)), dma((1,)),
         ],
         compiler_params=pltpu.CompilerParams(
             collective_id=0, has_side_effects=True, vmem_limit_bytes=60 * 1024 * 1024

time: 58.8 us -> 58.5 us (level)
  no operation moved by 1% of the time
where the time goes in v6:
time: 58.5 us; the launch traced here: 58.3 us
  Pallas kernels  55.8 us (95%)
  between operations  1.3 us (2%)
  local copies, waits for them, and re-layouts  1.25 us (2%)
    pallas_call x1, Pallas kernels, body(): pl.pallas_call(kernel, out_shape=jax.ShapeDtypeStruct((1, KBD, BLK), f32)...  55.8 us
    pallas_call x1, local copies, waits for them, and re-layouts, body(): pl.pallas_call(kernel, out_shape=jax.ShapeDtypeStruct((1, KBD, BLK), f32)...  1.25 us

profile of v6, /device:TPU:1, one launch (start us, length us, event | category | flops | bytes accessed | tf_op | source)
XLA Modules:
  0.0 58.3 jit_solution(15472780745874239859)
XLA Ops:
  1.3 55.8 %shard_map.55 = f32[1,3,128]{2,1,0:T(4,128)} custom-call(bf16[256,128]{1,0:T(8,128)(2,1)} %bitcast.3, bf16[384,128]{1,0:T(8,128)(2,1)} %bitcast.2, s32[1]{0:T(128)S(6)} %copy.7.pick_hbm, s32[1]{0:T(128)S(6)} %copy.8.off_hbm, s32[192]{0:T(256)} %own_hbm.1), custom_call_target="tpu_custom_call" | custom-call | flops 1610612736 | bytes 165000 | tf_op jit(solution)/shard_map/pallas_call | solution.py:528
  57.1 1.2 %copy.6 = f32[1,3,128]{2,0,1:T(1,128)} copy(f32[1,3,128]{2,1,0:T(4,128)} %shard_map.55) | data formatting | bytes 3072 | tf_op jit(solution)/shard_map/pallas_call | solution.py:528

commit v7 on v6

--- a/solution.py
+++ b/solution.py
@@ -206,9 +206,6 @@
     for c in range(CHUNKS):
         for direction in range(2):
             when(comes(direction, 2, z), trunk_copy(direction, 2, c).start)
-    for i in range(1, NH):
-        s1_copy(i).start()
-    serve_leaves(1)
     for copy in scalars:
         copy.wait()
     picked = (pick_ref[0] // (QH // KV)).astype(jnp.float32)
@@ -216,6 +213,9 @@
     picks[head] = pick_out[...]
     for i in range(1, NH):
         pk_copy(i).start()
+    for i in range(1, NH):
+        s1_copy(i).start()
+    serve_leaves(1)
     for side in range(2):
         signal(greet.at[0, side], at_z(z + 2 - 4 * side))
 

time: 58.5 us -> 58.3 us (level)
  no operation moved by 1% of the time
where the time goes in v7:
time: 58.3 us; the launch traced here: 58.1 us
  Pallas kernels  55.6 us (95%)
  between operations  1.3 us (2%)
  local copies, waits for them, and re-layouts  1.25 us (2%)
    pallas_call x1, Pallas kernels, body(): pl.pallas_call(kernel, out_shape=jax.ShapeDtypeStruct((1, KBD, BLK), f32)...  55.6 us
    pallas_call x1, local copies, waits for them, and re-layouts, body(): pl.pallas_call(kernel, out_shape=jax.ShapeDtypeStruct((1, KBD, BLK), f32)...  1.25 us

profile of v7, /device:TPU:1, one launch (start us, length us, event | category | flops | bytes accessed | tf_op | source)
XLA Modules:
  0.0 58.1 jit_solution(1789183865265200324)
XLA Ops:
  1.3 55.6 %shard_map.55 = f32[1,3,128]{2,1,0:T(4,128)} custom-call(bf16[256,128]{1,0:T(8,128)(2,1)} %bitcast.3, bf16[384,128]{1,0:T(8,128)(2,1)} %bitcast.2, s32[1]{0:T(128)S(6)} %copy.7.pick_hbm, s32[1]{0:T(128)S(6)} %copy.8.off_hbm, s32[192]{0:T(256)} %own_hbm.1), custom_call_target="tpu_custom_call" | custom-call | flops 1610612736 | bytes 165000 | tf_op jit(solution)/shard_map/pallas_call | solution.py:528
  56.9 1.2 %copy.6 = f32[1,3,128]{2,0,1:T(1,128)} copy(f32[1,3,128]{2,1,0:T(4,128)} %shard_map.55) | data formatting | bytes 3072 | tf_op jit(solution)/shard_map/pallas_call | solution.py:528
